TPU v7x, 512 devices: a whole 4x4x16 slice. The times are simulated.
512 devices in a mesh: fsdp: 64 (over x, z), tp: 8 (over y, core).
Axes of the slice: x: 4, y: 4, z: 16, core: 2. Of those that a mesh axis runs over, the one named last changes fastest.
Arguments:
- gradient: float32 [2, 8192, 8192], P(None, 'fsdp', 'tp'), may hold values from -16 to 16
- momentum: float32 [2, 8192, 8192], P(None, 'fsdp', 'tp'), may hold values from -6 to 6
- basis: float32 [2, 8192, 256], P(None, ('tp', 'fsdp')), may hold values from -1 to 1
Outputs:
- new_momentum: float32 [2, 8192, 8192], P(None, 'fsdp', 'tp')
- new_basis: float32 [2, 8192, 256], P(None, ('tp', 'fsdp'))
- update: float32 [2, 8192, 8192], P(None, 'fsdp', 'tp')
All inputs are finite; a program needn't handle non-finite values.
Results may differ from a plain program's by a relative error of at most 0.0003.
Values sent between devices are 32-bit elements; how exact they have to be, the bound alone decides.
A program may use at most 64 MiB of HBM per device.

v0:
```python
import math

import jax
import jax.numpy as jnp
from jax import lax
from jax.sharding import PartitionSpec as P

ROWS = 8192
COLS = 8192
RANK = 256
LAYERS = 2


keep_rate = 0.95
eps = 1e-06


def orthonormal(product):
    highest = lax.Precision.HIGHEST
    for sweep in range(2):
        local_gram = jnp.einsum(
            "kmi,kmj->kij", product, product, precision=highest, preferred_element_type=jnp.float32
        )
        gram = lax.psum(local_gram, "fsdp")
        factor = jnp.linalg.cholesky(gram)
        solved = jax.scipy.linalg.solve_triangular(factor, jnp.swapaxes(product, 1, 2), lower=True)
        product = jnp.swapaxes(solved, 1, 2)
    return product


def layer_step(gradient, momentum, basis):
    highest = lax.Precision.HIGHEST
    buffer = momentum + gradient
    share = basis.shape[1]
    partial_product = jnp.einsum(
        "kmc,kcj->kmj",
        buffer,
        lax.all_gather(basis, "fsdp", axis=1, tiled=True),
        precision=highest,
        preferred_element_type=jnp.float32,
    )
    product = lax.psum(partial_product, "tp")
    product = orthonormal(product)
    local_columns = jnp.einsum(
        "kmc,kmj->kcj", buffer, product, precision=highest, preferred_element_type=jnp.float32
    )
    column_block = lax.psum(local_columns, "fsdp")
    squares = lax.psum(jnp.sum(column_block * column_block, 1), "tp")
    normalized = column_block / jnp.sqrt(squares + eps)[:, None, :]
    first_row = lax.axis_index("fsdp") * share
    new_basis = lax.dynamic_slice_in_dim(normalized, first_row, share, 1)
    feedback = jnp.einsum(
        "kmj,kcj->kmc", product, column_block, precision=highest, preferred_element_type=jnp.float32
    )
    new_momentum = buffer - (1.0 - keep_rate) * feedback
    scale_factor = math.sqrt(ROWS * COLS / RANK)
    update = scale_factor * jnp.einsum(
        "kmj,kcj->kmc", product, normalized, precision=highest, preferred_element_type=jnp.float32
    )
    return (new_momentum, new_basis, update)


def per_device(gradient, momentum, basis):
    moms, bases, updates = ([], [], [])
    for layer in range(LAYERS):
        first, second, third = layer_step(
            gradient[layer : layer + 1], momentum[layer : layer + 1], basis[layer : layer + 1]
        )
        moms.append(first)
        bases.append(second)
        updates.append(third)
    return (jnp.concatenate(moms, 0), jnp.concatenate(bases, 0), jnp.concatenate(updates, 0))


def solution(mesh):
    return jax.shard_map(
        per_device,
        mesh=mesh,
        in_specs=(P(None, "fsdp", "tp"), P(None, "fsdp", "tp"), P(None, ("tp", "fsdp"), None)),
        out_specs=(P(None, "fsdp", "tp"), P(None, ("tp", "fsdp"), None), P(None, "fsdp", "tp")),
        check_vma=False,
    )
```

profile of v0, /device:TPU:1, one launch (start us, length us, event | category | flops | bytes accessed | tf_op | source)
XLA Modules:
  0.0 1459.7 jit_solution(9618958829459966421)
XLA Ops:
  7.2 1.3 fusion.65
  8.6 0.7 all-gather.5.cloned.1.call-update
  9.4 136.9 %all-gather.3.cloned.1.call-done = f32[1,1024,256]{2,1,0:T(8,128)} async-done(((f32[1,16,256]{2,1,0:T(8,128)}), f32[1,1024,256]{2,1,0:T(8,128)}) %all-gather.3.cloned.1.call-update) | async-done | bytes 1048592 | tf_op jit(solution)/shard_map/all_gather | solution.py:38
  146.3 2.9 convolution_bitcast_fusion.7
  149.2 135.7 %all-gather.5.cloned.1.call-done = f32[1,1024,256]{2,1,0:T(8,128)} async-done(((f32[1,16,256]{2,1,0:T(8,128)}), f32[1,1024,256]{2,1,0:T(8,128)}) %all-gather.5.cloned.1.call-update) | async-done | bytes 1048592 | tf_op jit(solution)/shard_map/all_gather | solution.py:38
  284.9 2.5 convolution_bitcast_fusion.6
  287.5 79.9 %all-reduce.17.cloned.1.call-done = (f32[1,128,256]{2,1,0:T(8,128)}, f32[1,128,256]{2,1,0:T(8,128)}) async-done(((f32[1,128,256]{2,1,0:T(8,128)}, f32[1,128,256]{2,1,0:T(8,128)}), (f32[1,128,256]{2,1,0:T(8,128)}, f32[1,128,256]{2,1,0:T(8,128)})) %all-reduce.17.cloned.1.call-update) | async-done | bytes 262160 | tf_op jit(solution)/shard_map/psum | solution.py:42
  367.4 2.1 convolution_bitcast_fusion.3
  369.5 1.1 convolution_bitcast_fusion.5
  370.9 257.5 %all-reduce.15.cloned.1.call-done = (f32[1,256,256]{1,2,0:T(8,128)}, f32[1,256,256]{1,2,0:T(8,128)}) async-done(((f32[1,256,256]{1,2,0:T(8,128)}, f32[1,256,256]{1,2,0:T(8,128)}), (f32[1,256,256]{1,2,0:T(8,128)}, f32[1,256,256]{1,2,0:T(8,128)})) %all-reduce.15.cloned.1.call-update) | async-done | bytes 524304 | tf_op jit(solution)/shard_map/psum | solution.py:24
  628.4 1.1 copy.11
  629.7 0.8 copy-done.8
  630.6 0.7 copy-done.10
  631.3 11.7 custom-call.33
  643.0 11.7 custom-call.25
  654.8 0.7 compare_reduce_fusion.7
  655.5 9.8 custom-call.26
  666.0 10.2 custom-call.34
  676.7 11.7 custom-call.35
  688.4 0.6 compare_reduce_fusion.2
  690.5 4.0 while.10
  691.1 1.4 bitcast_dynamic-update-slice_fusion.14
  693.1 1.4 bitcast_dynamic-update-slice_fusion.14
  694.5 19.7 %custom-call.36 = f32[2,128,128]{1,2,0:T(8,128)S(1)} custom-call(f32[2,128,128]{2,1,0:T(8,128)S(1)} %get-tuple-element.33), custom_call_target="InvertDiagBlocksLowerTriangular" | custom-call | tf_op jit(solution)/shard_map/jit(_solve_triangular)/triangular_solve | solution.py:26
  715.1 1.1 convolution_bitcast_fusion.2
  716.7 11.7 custom-call.27
  728.4 0.6 compare_reduce_fusion.6
  730.5 4.0 while.8
  731.1 1.4 bitcast_dynamic-update-slice_fusion.12
  733.1 1.4 bitcast_dynamic-update-slice_fusion.12
  734.5 19.7 %custom-call.28 = f32[2,128,128]{1,2,0:T(8,128)S(1)} custom-call(f32[2,128,128]{2,1,0:T(8,128)S(1)} %get-tuple-element.31), custom_call_target="InvertDiagBlocksLowerTriangular" | custom-call | tf_op jit(solution)/shard_map/jit(_solve_triangular)/triangular_solve | solution.py:26
  755.0 1.1 convolution_bitcast_fusion.4
  756.4 260.2 %all-reduce.13.cloned.1.call-done = (f32[1,256,256]{1,2,0:T(8,128)}, f32[1,256,256]{1,2,0:T(8,128)}) async-done(((f32[1,256,256]{1,2,0:T(8,128)}, f32[1,256,256]{1,2,0:T(8,128)}), (f32[1,256,256]{1,2,0:T(8,128)}, f32[1,256,256]{1,2,0:T(8,128)})) %all-reduce.13.cloned.1.call-update) | async-done | bytes 524304 | tf_op jit(solution)/shard_map/psum | solution.py:24
  1016.6 1.1 copy.13
  1017.8 11.7 custom-call.37
  1029.5 0.6 compare_reduce_fusion.1
  1030.2 9.8 custom-call.38
  1040.5 11.7 custom-call.39
  1052.3 0.6 compare_reduce_fusion
  1054.2 4.0 while.11
  1054.9 1.4 bitcast_dynamic-update-slice_fusion.15
  1056.9 1.4 bitcast_dynamic-update-slice_fusion.15
  1058.3 19.9 %custom-call.40 = f32[2,128,128]{1,2,0:T(8,128)S(1)} custom-call(f32[2,128,128]{2,1,0:T(8,128)S(1)} %get-tuple-element.34), custom_call_target="InvertDiagBlocksLowerTriangular" | custom-call | tf_op jit(solution)/shard_map/jit(_solve_triangular)/triangular_solve | solution.py:26
  1079.6 11.7 custom-call.29
  1091.3 0.6 compare_reduce_fusion.5
  1092.0 9.8 custom-call.30
  1102.3 11.7 custom-call.31
  1114.0 0.6 compare_reduce_fusion.4
  1116.0 4.0 while.9
  1116.7 1.4 bitcast_dynamic-update-slice_fusion.13
  1118.7 1.4 bitcast_dynamic-update-slice_fusion.13
  1120.1 19.9 %custom-call.32 = f32[2,128,128]{1,2,0:T(8,128)S(1)} custom-call(f32[2,128,128]{2,1,0:T(8,128)S(1)} %get-tuple-element.32), custom_call_target="InvertDiagBlocksLowerTriangular" | custom-call | tf_op jit(solution)/shard_map/jit(_solve_triangular)/triangular_solve | solution.py:26
  1140.8 2.0 convolution_bitcast_fusion.1
  1142.8 2.0 convolution_bitcast_fusion
  1144.8 273.3 %all-reduce.11.cloned.1.call-done = (f32[1,1024,256]{2,1,0:T(8,128)}, f32[1,1024,256]{2,1,0:T(8,128)}) async-done(((f32[1,1024,256]{2,1,0:T(8,128)}, f32[1,1024,256]{2,1,0:T(8,128)}), (f32[1,1024,256]{2,1,0:T(8,128)}, f32[1,1024,256]{2,1,0:T(8,128)})) %all-reduce.11.cloned.1.call-update) | async-done | bytes 2097168 | tf_op jit(solution)/shard_map/psum | solution.py:47
  1418.1 1.5 multiply_reduce_fusion
  1419.7 2.1 fusion.4
  1421.9 2.0 fusion.5
  1423.9 21.8 %all-reduce.4 = (f32[1,256]{1,0:T(1,128)S(1)}, f32[1,256]{1,0:T(1,128)S(1)}) all-reduce(f32[1,256]{1,0:T(1,128)S(1)} %bitcast.283, f32[1,256]{1,0:T(1,128)S(1)} %bitcast.285), channel_id=1, replica_groups=mesh['fsdp'=64,'tp'=8] {'tp'}, use_global_device_ids=true, to_apply=%region_15.18 | all-reduce | flops 512 | bytes 4096 | tf_op jit(solution)/shard_map/psum | solution.py:48
  1445.8 1.3 broadcast_divide_fusion
  1447.1 1.3 fusion.3
  1448.5 1.3 fusion.2
  1449.8 1.1 pad_maximum_fusion
  1450.9 1.1 pad_maximum_fusion.1
  (114 shorter events, 13.7 us)
Async XLA Ops:
  7.2 139.1 %all-gather.3.cloned.1.call-start = ((), (), s32[]{:S(2)}) async-start(), calls=%async_computation | async-start | bytes 1064960 | tf_op jit(solution)/shard_map/all_gather | solution.py:38
  8.6 276.3 %all-gather.5.cloned.1.call-start = ((), (), s32[]{:S(2)}) async-start(), calls=%async_computation.1 | async-start | bytes 1064960 | tf_op jit(solution)/shard_map/all_gather | solution.py:38
  9.3 275.5 %copy-start = (f32[2,128,1024]{2,1,0:T(8,128)S(1)}, f32[2,128,1024]{2,1,0:T(8,128)}, u32[]{:S(2)}) copy-start(f32[2,128,1024]{2,1,0:T(8,128)} %param.6) | copy-start | bytes 3145732
  9.3 275.5 %copy-start.1 = (f32[2,128,1024]{2,1,0:T(8,128)S(1)}, f32[2,128,1024]{2,1,0:T(8,128)}, u32[]{:S(2)}) copy-start(f32[2,128,1024]{2,1,0:T(8,128)} %param.7) | copy-start | bytes 3145732
  9.4 358.0 %all-reduce.17.cloned.1.call-start = ((), (), s32[]{:S(2)}) async-start(), calls=%async_computation.5 | async-start | bytes 524288 | tf_op jit(solution)/shard_map/psum | solution.py:42
  287.4 341.0 %all-reduce.15.cloned.1.call-start = ((), (), s32[]{:S(2)}) async-start(), calls=%async_computation.4 | async-start | bytes 1048576 | tf_op jit(solution)/shard_map/psum | solution.py:24
  367.4 2.1 copy-start.12
  370.6 645.9 %all-reduce.13.cloned.1.call-start = ((), (), s32[]{:S(2)}) async-start(), calls=%async_computation.3 | async-start | bytes 1048576 | tf_op jit(solution)/shard_map/psum | solution.py:24
  628.4 1.1 copy-start.9
  629.6 1.0 copy-start.8
  630.6 0.7 copy-start.10
  654.8 21.4 %copy-start.11 = (f32[1,256,256]{2,1,0:T(8,128)S(1)}, f32[1,256,256]{2,1,0:T(8,128)}, u32[]{:S(2)}) copy-start(f32[1,256,256]{2,1,0:T(8,128)} %copy-done.10) | copy-start | bytes 786436
  690.5 23.7 %copy-start.13 = (f32[1,128,256]{2,1,0:T(8,128)S(1)}, f32[1,128,256]{2,1,0:T(8,128)}, u32[]{:S(2)}) copy-start(f32[1,128,256]{2,1,0:T(8,128)} %get-tuple-element.75) | copy-start | bytes 393220
  756.1 662.0 %all-reduce.11.cloned.1.call-start = ((), (), s32[]{:S(2)}) async-start(), calls=%async_computation.2 | async-start | bytes 4194304 | tf_op jit(solution)/shard_map/psum | solution.py:47
  1016.6 1.2 copy-start.7
  1078.4 1.0 copy-start.6
  1418.1 1.5 copy-start.3
  1419.6 2.1 copy-start.2
  1448.5 1.3 copy-start.4
  1448.5 1.3 copy-start.5
Sparse Core Ops, SparseCore 0:
  11.5 134.7 all-gather.2
  149.8 135.0 all-gather.4
  287.8 79.4 all-reduce.16
  371.7 256.6 all-reduce.14
  756.3 260.2 all-reduce.12
  1144.9 273.1 all-reduce.10
where the time goes:
time: 1460 us
  waiting for transfers between devices  1140 us (78%)
  other arithmetic  224 us (15%)
  matrix products  26.5 us (2%)
  local copies, waits for them, and re-layouts  22 us (2%)
  blocking collectives  21.8 us (1%)
  between operations  20.2 us (1%)
    psum x2, waiting for transfers between devices, orthonormal(): gram = lax.psum(local_gram, 'fsdp')  518 us
    psum x1, waiting for transfers between devices, layer_step(): column_block = lax.psum(local_columns, 'fsdp')  273 us
    all_gather x2, waiting for transfers between devices, layer_step(): lax.all_gather(basis, 'fsdp', axis=1, tiled=True)  273 us
    another operation x28, other arithmetic, orthonormal(): factor = jnp.linalg.cholesky(gram)  139 us
    psum x1, waiting for transfers between devices, layer_step(): product = lax.psum(partial_product, 'tp')  79.9 us
    another operation x9, other arithmetic, orthonormal(): jax.scipy.linalg.solve_triangular(factor, jnp.swapaxes(product, 1, 2), lo...  79.3 us
  transfers between devices with their start and end apart: 6, of which 6 were waited for; matrix products, arithmetic and copies ran while one was open for 0% of the time, Pallas kernels for 0%

commit v1 on v0

v1 whole, which is shorter than its diff:
```python
import functools
import math

import jax
import jax.numpy as jnp
from jax import lax
from jax.experimental import pallas as pl
from jax.experimental.pallas import tpu as pltpu
from jax.sharding import PartitionSpec as P

ROWS = 8192
COLS = 8192
RANK = 256
LAYERS = 2
XS, ZS, YS, CS = 4, 16, 4, 2
TP = YS * CS
MESH = pl.DeviceIdType.MESH
HIGHEST = lax.Precision.HIGHEST
F32 = jnp.float32
BF16 = jnp.bfloat16
HALF = RANK // 2

keep_rate = 0.95
eps = 1e-06


def dot(a, b, dims):
    return lax.dot_general(a, b, (dims, ((), ())), precision=HIGHEST, preferred_element_type=F32)


class Place:
    def __init__(self):
        self.f = lax.axis_index("fsdp")
        self.t = lax.axis_index("tp")
        self.x = lax.div(self.f, ZS)
        self.z = lax.rem(self.f, ZS)
        self.y = lax.div(self.t, CS)
        self.c = lax.rem(self.t, CS)

    def zat(self, d):
        return lax.rem(self.z + (ZS + d), ZS)

    def xat(self, d):
        return lax.rem(self.x + (XS + d), XS)

    def yat(self, d):
        return lax.rem(self.y + (YS + d), YS)

    def zdev(self, d):
        return (self.x * ZS + self.zat(d), self.t)

    def xdev(self, d):
        return (self.xat(d) * ZS + self.z, self.t)

    def tdev(self, d):
        return (self.f, lax.rem(self.t + (TP + d), TP))

    def ydev(self, d):
        return (self.f, self.yat(d) * CS + self.c)

    def cdev(self):
        return (self.f, self.y * CS + (1 - self.c))


class Wires:
    def __init__(self, send, recv):
        self.send, self.recv, self.used = send, recv, 0
        self.sent = []

    def go(self, src, dst, device):
        i = self.used
        self.used += 1
        copy = pltpu.make_async_remote_copy(
            src_ref=src, dst_ref=dst, send_sem=self.send.at[i], recv_sem=self.recv.at[i],
            device_id=device, device_id_type=MESH,
        )
        copy.start()
        self.sent.append(copy)
        return copy

    def drain(self):
        for copy in self.sent:
            copy.wait_send()
        self.sent = []


def greet(devices):
    barrier = pltpu.get_barrier_semaphore()
    for device in devices:
        pl.semaphore_signal(barrier, inc=1, device_id=device, device_id_type=MESH)
    pl.semaphore_wait(barrier, len(devices))


def gather_plane(me, w, full):
    xa = [None] + [w.go(full.at[0, me.x, me.z], full.at[0, me.x, me.z], me.xdev(d)) for d in (1, 2, 3)]
    ring = {}
    plane = {}
    ahead = {}

    def spread(zd):
        block = full.at[1, me.x, me.zat(zd)]
        plane[zd] = [w.go(block, block, me.xdev(1)), w.go(block, block, me.xdev(-1))]

    def forward(zd):
        plane[zd][0].wait_recv()
        low = full.at[1, me.xat(-1), me.zat(zd), pl.ds(0, 8)]
        first = w.go(low, low, me.xdev(1))
        plane[zd][1].wait_recv()
        high = full.at[1, me.xat(1), me.zat(zd), pl.ds(8, 8)]
        ahead[zd] = [first, w.go(high, high, me.xdev(-1))]

    for s in range(9):
        for way, last in ((1, 8), (-1, 7)):
            if s > last:
                continue
            if s > 0:
                ring["b", way, s - 1].wait_recv()
            if s < last:
                block = full.at[1, me.x, me.zat(-way * s)]
                ring["b", way, s] = w.go(block, block, me.zdev(way))
        for zd in ([0] if s == 0 else [-s, s] if s < 8 else [-s]):
            spread(zd)
        for q in range(XS):
            for way, last in ((1, 8), (-1, 7)):
                if s > last:
                    continue
                if s == 0 and q > 0 and way == 1:
                    xa[q].wait_recv()
                if s > 0:
                    ring["a", way, s - 1, q].wait_recv()
                if s < last:
                    block = full.at[0, me.xat(-q), me.zat(-way * s)]
                    ring["a", way, s, q] = w.go(block, block, me.zdev(way))
        if s > 0:
            b = s - 1
            for zd in ([0] if b == 0 else [-b, b]):
                forward(zd)
    forward(-8)
    for pair in ahead.values():
        for copy in pair:
            copy.wait_recv()


def scatter_plane(me, w, part, full, rb0, xb0, rb1, half1, whole1):
    order = [8] + [d for s in range(7, 0, -1) for d in (s, -s)] + [0]
    slot = {d: i for i, d in enumerate(order)}
    first = {}
    for d in order:
        z = me.zat(d)
        i = slot[d]
        first[d] = [
            w.go(part.at[1, me.xat(2), z, pl.ds(0, 8)], half1.at[0, i], me.xdev(1)),
            w.go(part.at[1, me.xat(2), z, pl.ds(8, 8)], half1.at[1, i], me.xdev(-1)),
        ]
    second = {}

    def pass_on(d):
        z = me.zat(d)
        i = slot[d]
        first[d][0].wait_recv()
        part[1, me.xat(1), z, 0:8] = part[1, me.xat(1), z, 0:8] + half1[0, i]
        one = w.go(part.at[1, me.xat(1), z], whole1.at[0, i], me.xdev(1))
        first[d][1].wait_recv()
        part[1, me.xat(-1), z, 8:16] = part[1, me.xat(-1), z, 8:16] + half1[1, i]
        second[d] = [one, w.go(part.at[1, me.xat(-1), z], whole1.at[1, i], me.xdev(-1))]

    def collect(d):
        z = me.zat(d)
        i = slot[d]
        second[d][0].wait_recv()
        second[d][1].wait_recv()
        part[1, me.x, z] = part[1, me.x, z] + whole1[0, i] + whole1[1, i]

    def group(s):
        r = 8 - s
        return [8] if r == 8 else [0] if r == 0 else [r, -r]

    ring = {}
    for d in group(0):
        pass_on(d)
    for s in range(9):
        for q in range(XS):
            for k, (way, last) in enumerate(((1, 8), (-1, 7))):
                s0 = s - (8 - last)
                if s0 < 0 or s0 > last:
                    continue
                d = way * (last - s0)
                if s0 == 0:
                    ring["a", way, 0, q] = w.go(
                        part.at[0, q, me.zat(d)], rb0.at[k, 0, q], me.zdev(way))
                else:
                    ring["a", way, s0 - 1, q].wait_recv()
                    if s0 < last:
                        rb0[k, s0 - 1, q] = rb0[k, s0 - 1, q] + part[0, q, me.zat(d)]
                        ring["a", way, s0, q] = w.go(rb0.at[k, s0 - 1, q], rb0.at[k, s0, q], me.zdev(way))
        if s < 8:
            for d in group(s + 1):
                pass_on(d)
        for d in group(s):
            collect(d)
        for k, (way, last) in enumerate(((1, 8), (-1, 7))):
            s0 = s - (8 - last)
            if s0 < 0 or s0 > last:
                continue
            d = way * (last - s0)
            if s0 == 0:
                ring["b", way, 0] = w.go(part.at[1, me.x, me.zat(d)], rb1.at[k, 0], me.zdev(way))
            else:
                ring["b", way, s0 - 1].wait_recv()
                if s0 < last:
                    rb1[k, s0 - 1] = rb1[k, s0 - 1] + part[1, me.x, me.zat(d)]
                    ring["b", way, s0] = w.go(rb1.at[k, s0 - 1], rb1.at[k, s0], me.zdev(way))
    full[1, me.x, me.z] = part[1, me.x, me.z] + rb1[0, 7] + rb1[1, 6]
    for q in range(XS):
        rb0[0, 7, q] = rb0[0, 7, q] + part[0, q, me.z] + rb0[1, 6, q]
    copies = [w.go(rb0.at[0, 7, me.xat(d)], xb0.at[d], me.xdev(d)) for d in (1, 2, 3)]
    for copy in copies:
        copy.wait_recv()
    full[0, me.x, me.z] = rb0[0, 7, me.x] + xb0[1] + xb0[2] + xb0[3]


def sum_gram(me, w, product, gs, gfull, zbuf, xbuf, g_ref):
    gram = dot(product, product, ((0,), (0,)))
    for h in range(2):
        gs[h] = gram[:, h * HALF : (h + 1) * HALF].reshape(RANK // 8, 8, HALF)

    def tile(ref, z):
        return ref.at[lax.div(z, 8), me.y * 8 + lax.rem(z, 8)]

    copies = [w.go(tile(gs, me.zat(d)), zbuf.at[d], me.zdev(d)) for d in range(1, ZS)]
    total = gs[lax.div(me.z, 8), me.y * 8 + lax.rem(me.z, 8)]
    for d in range(1, ZS):
        copies[d - 1].wait_recv()
        total = total + zbuf[d]
    xbuf[me.x] = total
    copies = [w.go(xbuf.at[me.x], xbuf.at[me.x], me.xdev(d)) for d in range(1, XS)]
    for copy in copies:
        copy.wait_recv()
    gfull[lax.div(me.z, 8), me.y * 8 + lax.rem(me.z, 8)] = xbuf[0] + xbuf[1] + xbuf[2] + xbuf[3]
    copies = [w.go(tile(gfull, me.z), tile(gfull, me.z), me.zdev(d)) for d in range(1, ZS)]
    for copy in copies:
        copy.wait_recv()
    mine = gfull.at[:, pl.ds(me.y * 8, 8)]
    copies = [w.go(mine, mine, me.ydev(d)) for d in range(1, YS)]
    for copy in copies:
        copy.wait_recv()
    for h in range(2):
        g_ref[:, h * HALF : (h + 1) * HALF] = gfull[h].reshape(RANK, HALF)


def first_kernel(grad, mom, basis, p_ref, g_ref, gbuf, mbuf, full, part, rs, gs, gfull, zbuf, xbuf, send, recv, local):
    me = Place()
    w = Wires(send, recv)
    loads = [pltpu.make_async_copy(grad, gbuf, local.at[0]), pltpu.make_async_copy(mom, mbuf, local.at[1])]
    for load in loads:
        load.start()
    full[0, me.x, me.z] = basis[0]
    full[1, me.x, me.z] = basis[1]
    greet([me.zdev(d) for d in range(1, ZS)] + [me.xdev(d) for d in range(1, XS)] + [me.tdev(d) for d in range(1, TP)])
    gather_plane(me, w, full)
    for load in loads:
        load.wait()
    share = part.shape[2]
    for l in range(LAYERS):
        total = jnp.zeros((part.shape[1] * share, RANK), F32)
        for x in range(XS):
            cols = pl.ds(x * 256, 256)
            total = total + dot(
                mbuf[l, :, cols] + gbuf[l, :, cols], full[l, x].reshape(256, RANK), ((1,), (0,)))
        part[l] = total.reshape(part.shape[1], share, RANK)
    copies = []
    for d in range(1, TP):
        there = lax.rem(me.t + d, TP)
        copies.append(w.go(part.at[lax.rem(there, CS), lax.div(there, CS)], rs.at[d], me.tdev(d)))
    total = part[me.c, me.y]
    for d in range(1, TP):
        copies[d - 1].wait_recv()
        total = total + rs[d]
    rows = pl.ds(me.y * share, share)
    p_ref[rows] = total
    copies = [w.go(p_ref.at[rows], p_ref.at[rows], me.ydev(d)) for d in range(1, YS)]
    for copy in copies:
        copy.wait_recv()
    sum_gram(me, w, p_ref[...], gs, gfull, zbuf, xbuf, g_ref)
    w.drain()


def second_kernel(p, inv, p_ref, g_ref, gs, gfull, zbuf, xbuf, send, recv):
    me = Place()
    w = Wires(send, recv)
    p_ref[...] = dot(p[...], inv[...], ((1,), (1,)))
    greet([me.zdev(d) for d in range(1, ZS)] + [me.xdev(d) for d in range(1, XS)] + [me.ydev(d) for d in range(1, YS)])
    sum_gram(me, w, p_ref[...], gs, gfull, zbuf, xbuf, g_ref)
    w.drain()


def last_kernel(grad, mom, p, inv, new_mom, new_basis, update,
                gbuf, mbuf, q, part, full, rb0, xb0, rb1, half1, whole1, sq, send, recv, local):
    me = Place()
    w = Wires(send, recv)
    loads = [pltpu.make_async_copy(grad, gbuf, local.at[0]), pltpu.make_async_copy(mom, mbuf, local.at[1])]
    for load in loads:
        load.start()
    q[me.c] = dot(p[...], inv[...], ((1,), (1,)))
    greet([me.zdev(1), me.zdev(-1)] + [me.xdev(d) for d in range(1, XS)] + [me.tdev(d) for d in range(1, TP)])
    swap = w.go(q.at[me.c], q.at[me.c], me.cdev())
    for load in loads:
        load.wait()
    gbuf[...] = gbuf[...] + mbuf[...]
    swap.wait_recv()
    for l in range(LAYERS):
        for x in range(XS):
            cols = dot(gbuf[l, :, pl.ds(x * 256, 256)], q[l], ((0,), (0,)))
            part[l, x] = cols.reshape(ZS, 16, RANK)
    scatter_plane(me, w, part, full, rb0, xb0, rb1, half1, whole1)
    gather_plane(me, w, full)
    for l in range(LAYERS):
        squares = jnp.zeros((1, RANK), F32)
        for x in range(XS):
            block = full[l, x].reshape(256, RANK)
            squares = squares + jnp.sum(block * block, 0, keepdims=True)
        sq[me.t, l] = jnp.broadcast_to(squares, (8, RANK))
    copies = [w.go(sq.at[me.t], sq.at[me.t], me.tdev(d)) for d in range(1, TP)]
    for l in range(LAYERS):
        for x in range(XS):
            block = full[l, x].reshape(256, RANK)
            cols = pl.ds(x * 256, 256)
            new_mom[l, :, cols] = gbuf[l, :, cols] - (1.0 - keep_rate) * dot(q[l], block, ((1,), (1,)))
    for copy in copies:
        copy.wait_recv()
    for l in range(LAYERS):
        squares = sq[0, l]
        for t in range(1, TP):
            squares = squares + sq[t, l]
        norm = jnp.sqrt(squares[0:1] + eps)
        new_basis[l] = full[l, me.x, me.z] / norm
        scaled = q[l] * (math.sqrt(ROWS * COLS / RANK) / norm)
        for x in range(XS):
            block = full[l, x].reshape(256, RANK)
            update[l, :, pl.ds(x * 256, 256)] = dot(scaled, block, ((1,), (1,)))
    w.drain()


def split3(a):
    high = a.astype(BF16)
    rest = a - high.astype(F32)
    mid = rest.astype(BF16)
    low = (rest - mid.astype(F32)).astype(BF16)
    return high, mid, low


def eliminate(a_ref, w_ref):
    b = 32
    lanes = lax.broadcasted_iota(jnp.int32, (b, RANK), 1)
    rows = lax.broadcasted_iota(jnp.int32, (b, RANK), 0)
    row_index = lax.broadcasted_iota(jnp.int32, (b, 1), 0)
    for r0 in range(0, RANK, b):
        panel = a_ref[r0 : r0 + b, :]
        scale = jnp.zeros((b, 1), F32)
        for k in range(b):
            j = r0 + k
            col = panel[:, j : j + 1]
            pivot = panel[k : k + 1, j : j + 1]
            scale = jnp.where(row_index == k, lax.rsqrt(pivot), scale)
            ratio = jnp.where(row_index > k, col * (1.0 / pivot), 0.0)
            at = lanes == j
            row = jnp.where(at[0:1], 1.0, panel[k : k + 1, :])
            kept = jnp.where(at & (rows >= k), jnp.where(rows == k, 1.0, 0.0), panel)
            panel = kept - ratio * row
        panel = panel * scale
        done = lanes <= rows + r0
        w_ref[r0 : r0 + b, :] = jnp.where(done, panel, 0.0)
        if r0 + b < RANK:
            inner = (lanes >= r0) & (lanes < r0 + b) & (lanes > rows + r0)
            right = jnp.where(inner, 0.0, panel)
            h, m, l = split3(panel)
            hr, mr, lr = split3(right)
            left6 = jnp.concatenate([h, h, m, h, l, m], 0)
            right6 = jnp.concatenate([hr, mr, hr, lr, hr, mr], 0)
            rest = RANK - r0 - b
            change = lax.dot_general(
                left6, right6, (((0,), (0,)), ((), ())), preferred_element_type=F32)
            all_lanes = lax.broadcasted_iota(jnp.int32, (rest, RANK), 1)
            old = jnp.where((all_lanes >= r0) & (all_lanes < r0 + b), 0.0, a_ref[r0 + b :, :])
            a_ref[r0 + b :, :] = old - change[r0 + b :, :]


def factor_kernel(g, w_ref, a):
    a[...] = g[...]
    eliminate(a, w_ref)


def vmem(*shape):
    return pltpu.VMEM(shape, F32)


def params(collective_id):
    return pltpu.CompilerParams(collective_id=collective_id, has_side_effects=True, vmem_limit_bytes=48 * 2**20)


V = pl.BlockSpec(memory_space=pltpu.VMEM)
ANY = pl.BlockSpec(memory_space=pl.ANY)


def sums(n):
    return [
        vmem(2, RANK // 8, 8, HALF), vmem(2, RANK // 8, 8, HALF), vmem(ZS, 8, HALF), vmem(XS, 8, HALF),
        pltpu.SemaphoreType.DMA((n,)), pltpu.SemaphoreType.DMA((n,)),
    ]


def per_device(gradient, momentum, basis):
    rows, cols = gradient.shape[1:]
    share = basis.shape[1]
    small = jax.ShapeDtypeStruct((RANK, RANK), F32)
    tall = jax.ShapeDtypeStruct((rows, RANK), F32)
    product, gram = pl.pallas_call(
        first_kernel,
        out_shape=(tall, small),
        in_specs=[ANY, ANY, V],
        out_specs=(V, V),
        scratch_shapes=[
            vmem(LAYERS, rows, cols), vmem(LAYERS, rows, cols), vmem(LAYERS, XS, ZS, share, RANK),
            vmem(LAYERS, YS, rows // YS, RANK), vmem(TP, rows // YS, RANK),
        ] + sums(240) + [pltpu.SemaphoreType.DMA((2,))],
        compiler_params=params(0),
        name="first",
    )(gradient, momentum, basis)
    factor = pl.pallas_call(
        factor_kernel, out_shape=small, in_specs=[V], out_specs=V, scratch_shapes=[vmem(RANK, RANK)],
        compiler_params=pltpu.CompilerParams(vmem_limit_bytes=32 * 2**20), name="factor")
    inverse = factor(gram)
    product, gram = pl.pallas_call(
        second_kernel,
        out_shape=(tall, small),
        in_specs=[V, V],
        out_specs=(V, V),
        scratch_shapes=sums(40),
        compiler_params=params(1),
        name="second",
    )(product, inverse)
    inverse = factor(gram)
    whole = jax.ShapeDtypeStruct((LAYERS, rows, cols), F32)
    return pl.pallas_call(
        last_kernel,
        out_shape=(whole, jax.ShapeDtypeStruct((LAYERS, share, RANK), F32), whole),
        in_specs=[ANY, ANY, V, V],
        out_specs=(V, V, V),
        scratch_shapes=[
            vmem(LAYERS, rows, cols), vmem(LAYERS, rows, cols), vmem(LAYERS, rows, RANK),
            vmem(LAYERS, XS, ZS, share, RANK), vmem(LAYERS, XS, ZS, share, RANK),
            vmem(2, 8, XS, share, RANK), vmem(XS, share, RANK), vmem(2, 8, share, RANK),
            vmem(2, ZS, 8, RANK), vmem(2, ZS, share, RANK), vmem(TP, LAYERS, 8, RANK),
            pltpu.SemaphoreType.DMA((320,)), pltpu.SemaphoreType.DMA((320,)), pltpu.SemaphoreType.DMA((2,)),
        ],
        compiler_params=params(2),
        name="last",
    )(gradient, momentum, product, inverse)


def solution(mesh):
    return jax.shard_map(
        per_device,
        mesh=mesh,
        in_specs=(P(None, "fsdp", "tp"), P(None, "fsdp", "tp"), P(None, ("tp", "fsdp"), None)),
        out_specs=(P(None, "fsdp", "tp"), P(None, ("tp", "fsdp"), None), P(None, "fsdp", "tp")),
        check_vma=False,
    )
```

time: 1460 us -> 260 us (0.18)
  waiting for transfers between devices: 1140 us -> 0 us
  Pallas kernels: 0 us -> 254 us
  other arithmetic: 224 us -> 0 us
  matrix products: 26.5 us -> 0 us
  blocking collectives: 21.8 us -> 0 us
  between operations: 20.2 us -> 0.68 us
  local copies, waits for them, and re-layouts: 22 us -> 5.76 us
    psum x4 -> x0, waiting for transfers between devices: 871 us -> none  [the longest x2 518 us: orthonormal(): gram = lax.psum(local_gram, 'fsdp')]
    all_gather x2 -> x0, waiting for transfers between devices: 273 us -> none  [layer_step(): lax.all_gather(basis, 'fsdp', axis=1, tiled=True)]
    pallas_call x0 -> x5, Pallas kernels: none -> 254 us  [the longest x1 95.6 us: per_device(): pl.pallas_call(last_kernel, out_shape=(whole, jax.ShapeDtypeStruct((LAYER...]
    another operation x37 -> x0, other arithmetic: 218 us -> none  [the longest x28 139 us: orthonormal(): factor = jnp.linalg.cholesky(gram)]
    psum x1 -> x0, blocking collectives: 21.8 us -> none  [layer_step(): squares = lax.psum(jnp.sum(column_block * column_block, 1), 'tp')]
    dot_general x12 -> x0, matrix products: 21.4 us -> none  [the longest x4 5.4 us: orthonormal(): jnp.einsum('kmi,kmj->kij', product, product, precision=highest, preferred...]
    another operation x37 -> x0, local copies, waits for them, and re-layouts: 16 us -> none  [the longest x29 15.9 us: orthonormal(): jax.scipy.linalg.solve_triangular(factor, jnp.swapaxes(product, 1, 2), lo...]
  transfers between devices with their start and end apart: 6 -> 0, of which waited for: 6 -> 0; matrix products, arithmetic and copies ran while one was open for 0% -> 0% of each run, Pallas kernels for 0% -> 0%
where the time goes in v1:
time: 260 us
  Pallas kernels  254 us (98%)
  local copies, waits for them, and re-layouts  5.76 us (2%)
    pallas_call x1, Pallas kernels, per_device(): pl.pallas_call(last_kernel, out_shape=(whole, jax.ShapeDtypeStruct((LAYER...  95.6 us
    pallas_call x1, Pallas kernels, per_device(): pl.pallas_call(first_kernel, out_shape=(tall, small), in_specs=[ANY, ANY,...  84.4 us
    pallas_call x2, Pallas kernels, per_device(): inverse = factor(gram)  47 us
    pallas_call x1, Pallas kernels, per_device(): pl.pallas_call(second_kernel, out_shape=(tall, small), in_specs=[V, V], o...  26.6 us
    unnamed x11, local copies, waits for them, and re-layouts  5.76 us

profile of v1, /device:TPU:1, one launch (start us, length us, event | category | flops | bytes accessed | tf_op | source)
XLA Modules:
  0.0 260.1 jit_solution(13840234384125582639)
XLA Ops:
  0.6 0.0 copy-start
  0.6 1.2 copy-done
  1.9 0.0 copy-start.2
  1.9 1.2 copy-done.2
  3.1 0.0 copy-start.3
  3.1 0.8 copy-done.3
  3.8 84.4 %first.1 = (f32[128,256]{1,0:T(8,128)S(1)}, f32[256,256]{1,0:T(8,128)S(1)}) custom-call(f32[2,128,1024]{2,1,0:T(8,128)S(1)} %copy-done, f32[2,128,1024]{2,1,0:T(8,128)S(1)} %copy-done.2, f32[2,16,256]{2,1,0:T(8,128)S(1)} %copy-done.3), custom_call_target="tpu_custom_call" | custom-call | tf_op jit(solution)/shard_map/first/pallas_call | solution.py:417
  88.3 0.0 copy-start.1
  88.3 23.5 %factor.2.inv = f32[256,256]{1,0:T(8,128)S(1)} custom-call(f32[256,256]{1,0:T(8,128)S(1)} %get-tuple-element.8.g), custom_call_target="tpu_custom_call" | custom-call | tf_op jit(solution)/shard_map/factor/pallas_call | solution.py:432
  111.7 26.6 %second.1 = (f32[128,256]{1,0:T(8,128)S(1)}, f32[256,256]{1,0:T(8,128)S(1)}) custom-call(f32[128,256]{1,0:T(8,128)S(1)} %get-tuple-element.7.p, f32[256,256]{1,0:T(8,128)S(1)} %factor.2.inv), custom_call_target="tpu_custom_call" | custom-call | tf_op jit(solution)/shard_map/second/pallas_call | solution.py:433
  138.3 23.6 %factor.3.inv = f32[256,256]{1,0:T(8,128)S(1)} custom-call(f32[256,256]{1,0:T(8,128)S(1)} %get-tuple-element.10.g), custom_call_target="tpu_custom_call" | custom-call | tf_op jit(solution)/shard_map/factor/pallas_call | solution.py:442
  161.9 0.0 copy-done.1
  161.9 95.6 %last.1 = (f32[2,128,1024]{2,1,0:T(8,128)S(1)}, f32[2,16,256]{2,1,0:T(8,128)S(1)}, f32[2,128,1024]{2,1,0:T(8,128)S(1)}) custom-call(f32[2,128,1024]{2,1,0:T(8,128)S(1)} %copy-done.1, f32[2,128,1024]{2,1,0:T(8,128)S(1)} %copy-done.2, f32[128,256]{1,0:T(8,128)S(1)} %get-tuple-element.9.p, f32[256,256]{1,0:T(8,128)S(1)} %factor.3.inv), custom_call_target="tpu_custom_call" | custom-call | tf_op jit(solution)/shard_map/last/pallas_call | solution.py:444
  257.5 1.0 copy.9
  258.5 0.6 copy.10
  259.1 1.0 copy.11
Async XLA Ops:
  0.6 1.2 copy-start
  1.9 1.2 copy-start.2
  3.1 0.8 copy-start.3
  88.3 73.6 %copy-start.1 = (f32[2,128,1024]{2,1,0:T(8,128)S(1)}, f32[2,128,1024]{2,1,0:T(8,128)}, u32[]{:S(2)}) copy-start(f32[2,128,1024]{2,1,0:T(8,128)} %grad.3) | copy-start | bytes 3145732

commit v2 on v1

v2 whole, which is shorter than its diff:
```python
import functools
import math

import jax
import jax.numpy as jnp
from jax import lax
from jax.experimental import pallas as pl
from jax.experimental.pallas import tpu as pltpu
from jax.sharding import PartitionSpec as P

ROWS = 8192
COLS = 8192
RANK = 256
LAYERS = 2
XS, ZS, YS, CS = 4, 16, 4, 2
TP = YS * CS
MESH = pl.DeviceIdType.MESH
HIGHEST = lax.Precision.HIGHEST
F32 = jnp.float32
BF16 = jnp.bfloat16
HALF = RANK // 2

keep_rate = 0.95
eps = 1e-06


def dot(a, b, dims):
    return lax.dot_general(a, b, (dims, ((), ())), precision=HIGHEST, preferred_element_type=F32)


def split2(a):
    high = a.astype(BF16)
    return high, (a - high.astype(F32)).astype(BF16)


def dot3(a, b, axis):
    ah, al = split2(a)
    bh, bl = split2(b)
    return lax.dot_general(
        jnp.concatenate([ah, ah, al], axis), jnp.concatenate([bh, bl, bh], axis),
        (((axis,), (axis,)), ((), ())), preferred_element_type=F32)


class Place:
    def __init__(self):
        self.f = lax.axis_index("fsdp")
        self.t = lax.axis_index("tp")
        self.x = lax.div(self.f, ZS)
        self.z = lax.rem(self.f, ZS)
        self.y = lax.div(self.t, CS)
        self.c = lax.rem(self.t, CS)

    def zat(self, d):
        return lax.rem(self.z + (ZS + d), ZS)

    def xat(self, d):
        return lax.rem(self.x + (XS + d), XS)

    def yat(self, d):
        return lax.rem(self.y + (YS + d), YS)

    def cols(self, e):
        return pl.ds(pl.multiple_of(self.xat(e) * 256, 256), 256)

    def zdev(self, d):
        return (self.x * ZS + self.zat(d), self.t)

    def xdev(self, d):
        return (self.xat(d) * ZS + self.z, self.t)

    def tdev(self, d):
        return (self.f, lax.rem(self.t + (TP + d), TP))

    def ydev(self, d):
        return (self.f, self.yat(d) * CS + self.c)

    def cdev(self):
        return (self.f, self.y * CS + (1 - self.c))


class Wires:
    def __init__(self, send, recv):
        self.send, self.recv, self.used = send, recv, 0
        self.sent = []

    def go(self, src, dst, device):
        i = self.used
        self.used += 1
        copy = pltpu.make_async_remote_copy(
            src_ref=src, dst_ref=dst, send_sem=self.send.at[i], recv_sem=self.recv.at[i],
            device_id=device, device_id_type=MESH,
        )
        copy.start()
        self.sent.append(copy)
        return copy

    def drain(self):
        for copy in self.sent:
            copy.wait_send()
        self.sent = []


def gathered(full0, full1, l, e):
    block = full0[:, e] if l == 0 else full1[e]
    return block.reshape(256, RANK)


def greet(devices):
    barrier = pltpu.get_barrier_semaphore()
    for device in devices:
        pl.semaphore_signal(barrier, inc=1, device_id=device, device_id_type=MESH)
    pl.semaphore_wait(barrier, len(devices))


WAYS = ((1, 8), (-1, 7))


def near(way, d):
    return 0 if d == 0 else 2 * d - 1 if way == 1 else 2 * d


def offset(slot):
    return 0 if slot == 0 else -((slot + 1) // 2) if slot % 2 else slot // 2


GROUPS = ((0, 5), (5, 9), (9, 13), (13, 16))


def gather_plane(me, w, own0, own1, full0, slots1, full1):
    full0[me.z, 0] = own0
    slots1[0, 0] = own1
    full1[0, me.z] = own1
    xa = {e: w.go(full0.at[me.z, 0], full0.at[me.z, (-e) % XS], me.xdev(e)) for e in (3, 1, 2)}
    ring, wide, ahead = {}, {}, {}

    def hop_b(s):
        for way, last in WAYS:
            if 0 < s <= last:
                ring["b", way, s - 1].wait_recv()
            if s < last:
                ring["b", way, s] = w.go(
                    slots1.at[0, near(way, s)], slots1.at[0, near(way, s + 1)], me.zdev(way))

    def hop_a(s):
        for half in (0, 1):
            pair = pl.ds(2 * half, 2)
            for way, last in WAYS:
                if s == 0 and way == 1:
                    for e in ((3,), (1, 2))[half]:
                        xa[e].wait_recv()
                if 0 < s <= last:
                    ring["a", way, s - 1, half].wait_recv()
                if s < last:
                    block = full0.at[me.zat(-way * s), pair]
                    ring["a", way, s, half] = w.go(block, block, me.zdev(way))

    def spread(g):
        lo, hi = GROUPS[g]
        group = slots1.at[0, pl.ds(lo, hi - lo)]
        wide[g] = [w.go(group, slots1.at[(-e) % XS, pl.ds(lo, hi - lo)], me.xdev(e)) for e in (1, -1)]
        for i in range(lo, hi):
            full1[0, me.zat(offset(i))] = slots1[0, i]

    def forward(g):
        lo, hi = GROUPS[g]
        mid = (lo + hi) // 2
        ahead[g] = []
        for n, (a, b, e) in enumerate(((lo, mid, 1), (mid, hi, -1))):
            wide[g][n].wait_recv()
            ahead[g].append(
                w.go(slots1.at[(-e) % XS, pl.ds(a, b - a)], slots1.at[2, pl.ds(a, b - a)], me.xdev(e)))
        for i in range(lo, hi):
            for e in (1, 3):
                full1[e, me.zat(offset(i))] = slots1[e, i]

    for s in range(9):
        hop_b(s)
        if s in (2, 4, 6, 8):
            spread(s // 2 - 1)
        hop_a(s)
        if s in (4, 6, 8):
            forward(s // 2 - 2)
    forward(3)
    for g in range(4):
        for copy in ahead[g]:
            copy.wait_recv()
        for i in range(*GROUPS[g]):
            full1[2, me.zat(offset(i))] = slots1[2, i]


FAR = [8] + [d for r in range(7, 0, -1) for d in (r, -r)] + [0]
FAR_GROUPS = ((0, 3), (3, 7), (7, 11), (11, 16))


def scatter_plane(me, w, part0, part1, rb0, xb0, rb1, half1, whole1):
    first, second, ring = {}, {}, {}

    def begin(g):
        lo, hi = FAR_GROUPS[g]
        mid = (lo + hi) // 2
        first[g] = [
            w.go(part1.at[2, pl.ds(a, b - a)], half1.at[pl.ds(a, b - a)], me.xdev(e))
            for a, b, e in ((lo, mid, 1), (mid, hi, -1))
        ]

    def pass_on(g):
        lo, hi = FAR_GROUPS[g]
        mid = (lo + hi) // 2
        second[g] = []
        for n, (a, b, e) in enumerate(((lo, mid, 1), (mid, hi, -1))):
            first[g][n].wait_recv()
            part1[e % XS, a:b] = part1[e % XS, a:b] + half1[a:b]
            second[g].append(
                w.go(part1.at[e % XS, pl.ds(lo, hi - lo)], whole1.at[n, pl.ds(lo, hi - lo)], me.xdev(e)))

    def collect(g):
        lo, hi = FAR_GROUPS[g]
        for copy in second[g]:
            copy.wait_recv()
        part1[0, lo:hi] = part1[0, lo:hi] + whole1[0, lo:hi] + whole1[1, lo:hi]

    def hop_a(s):
        for half in (0, 1):
            lo, hi = 2 * half, 2 * half + 2
            pair = pl.ds(lo, 2)
            for k, (way, last) in enumerate(WAYS):
                if s > last:
                    continue
                there = me.zat(way * (last - s))
                if s == 0:
                    ring["a", way, 0, half] = w.go(part0.at[there, pair], rb0.at[k, 0, pair], me.zdev(way))
                    continue
                ring["a", way, s - 1, half].wait_recv()
                if s < last:
                    rb0[k, s - 1, lo:hi] = rb0[k, s - 1, lo:hi] + part0[there, lo:hi]
                    ring["a", way, s, half] = w.go(rb0.at[k, s - 1, pair], rb0.at[k, s, pair], me.zdev(way))

    def hop_b(s):
        for k, (way, last) in enumerate(WAYS):
            if s > last:
                continue
            slot = FAR.index(way * (last - s))
            if s == 0:
                ring["b", way, 0] = w.go(part1.at[0, slot], rb1.at[k, 0], me.zdev(way))
                continue
            ring["b", way, s - 1].wait_recv()
            if s < last:
                rb1[k, s - 1] = rb1[k, s - 1] + part1[0, slot]
                ring["b", way, s] = w.go(rb1.at[k, s - 1], rb1.at[k, s], me.zdev(way))

    for g in range(4):
        begin(g)
    copies = []
    for s in range(11):
        if s <= 8:
            hop_a(s)
        if s == 8:
            rb0[0, 7] = rb0[0, 7] + part0[me.z] + rb0[1, 6]
            copies = [w.go(rb0.at[0, 7, e], xb0.at[e], me.xdev(e)) for e in (2, 1, 3)]
        if s in (0, 2, 4, 6):
            pass_on(s // 2)
        if s in (1, 3, 5, 7):
            collect(s // 2)
        if s >= 2:
            hop_b(s - 2)
    for copy in copies:
        copy.wait_recv()
    return rb0[0, 7, 0] + xb0[1] + xb0[2] + xb0[3], part1[0, 15] + rb1[0, 7] + rb1[1, 6]


def sum_gram(me, w, product, gs, gfull, zbuf, xbuf, g_ref):
    gram = dot(product, product, ((0,), (0,)))
    for h in range(2):
        gs[h] = gram[:, h * HALF : (h + 1) * HALF].reshape(RANK // 8, 8, HALF)

    def tile(ref, z):
        return ref.at[lax.div(z, 8), me.y * 8 + lax.rem(z, 8)]

    copies = [w.go(tile(gs, me.zat(d)), zbuf.at[d], me.zdev(d)) for d in range(1, ZS)]
    total = gs[lax.div(me.z, 8), me.y * 8 + lax.rem(me.z, 8)]
    for d in range(1, ZS):
        copies[d - 1].wait_recv()
        total = total + zbuf[d]
    xbuf[me.x] = total
    copies = [w.go(xbuf.at[me.x], xbuf.at[me.x], me.xdev(d)) for d in range(1, XS)]
    for copy in copies:
        copy.wait_recv()
    gfull[lax.div(me.z, 8), me.y * 8 + lax.rem(me.z, 8)] = xbuf[0] + xbuf[1] + xbuf[2] + xbuf[3]
    copies = [w.go(tile(gfull, me.z), tile(gfull, me.z), me.zdev(d)) for d in range(1, ZS)]
    for copy in copies:
        copy.wait_recv()
    mine = gfull.at[:, pl.ds(me.y * 8, 8)]
    copies = [w.go(mine, mine, me.ydev(d)) for d in range(1, YS)]
    for copy in copies:
        copy.wait_recv()
    for h in range(2):
        g_ref[:, h * HALF : (h + 1) * HALF] = gfull[h].reshape(RANK, HALF)


def first_kernel(grad, mom, basis, p_ref, g_ref, gbuf, mbuf, full0, slots1, full1, part, rs, gs, gfull, zbuf, xbuf, send, recv, local):
    me = Place()
    w = Wires(send, recv)
    loads = [pltpu.make_async_copy(grad, gbuf, local.at[0]), pltpu.make_async_copy(mom, mbuf, local.at[1])]
    for load in loads:
        load.start()
    greet([me.zdev(d) for d in range(1, ZS)] + [me.xdev(d) for d in range(1, XS)] + [me.tdev(d) for d in range(1, TP)])
    gather_plane(me, w, basis[0], basis[1], full0, slots1, full1)
    for load in loads:
        load.wait()
    share = part.shape[2]
    for l in range(LAYERS):
        total = jnp.zeros((part.shape[1] * share, RANK), F32)
        for e in range(XS):
            cols = me.cols(e)
            total = total + dot(
                mbuf[l, :, cols] + gbuf[l, :, cols], gathered(full0, full1, l, e), ((1,), (0,)))
        part[l] = total.reshape(part.shape[1], share, RANK)
    copies = []
    for d in range(1, TP):
        there = lax.rem(me.t + d, TP)
        copies.append(w.go(part.at[lax.rem(there, CS), lax.div(there, CS)], rs.at[d], me.tdev(d)))
    total = part[me.c, me.y]
    for d in range(1, TP):
        copies[d - 1].wait_recv()
        total = total + rs[d]
    rows = pl.ds(me.y * share, share)
    p_ref[rows] = total
    copies = [w.go(p_ref.at[rows], p_ref.at[rows], me.ydev(d)) for d in range(1, YS)]
    for copy in copies:
        copy.wait_recv()
    sum_gram(me, w, p_ref[...], gs, gfull, zbuf, xbuf, g_ref)
    w.drain()


def second_kernel(p, inv, p_ref, g_ref, gs, gfull, zbuf, xbuf, send, recv):
    me = Place()
    w = Wires(send, recv)
    p_ref[...] = dot(p[...], inv[...], ((1,), (1,)))
    greet([me.zdev(d) for d in range(1, ZS)] + [me.xdev(d) for d in range(1, XS)] + [me.ydev(d) for d in range(1, YS)])
    sum_gram(me, w, p_ref[...], gs, gfull, zbuf, xbuf, g_ref)
    w.drain()


def last_kernel(grad, mom, p, inv, new_mom, new_basis, update,
                gbuf, mbuf, q, part0, part1, tmp, full0, slots1, full1, rb0, xb0, rb1, half1, whole1, sq,
                send, recv, local):
    me = Place()
    w = Wires(send, recv)
    loads = [pltpu.make_async_copy(grad, gbuf, local.at[0]), pltpu.make_async_copy(mom, mbuf, local.at[1])]
    for load in loads:
        load.start()
    q[me.c] = dot(p[...], inv[...], ((1,), (1,)))
    greet([me.zdev(1), me.zdev(-1)] + [me.xdev(d) for d in range(1, XS)] + [me.tdev(d) for d in range(1, TP)])
    swap = w.go(q.at[me.c], q.at[me.c], me.cdev())
    for load in loads:
        load.wait()
    gbuf[...] = gbuf[...] + mbuf[...]
    swap.wait_recv()
    for e in (2, 1, 3, 0):
        tmp[...] = dot3(gbuf[1, :, me.cols(e)], q[1], 0).reshape(ZS, 16, RANK)
        for slot, d in enumerate(FAR):
            part1[e, slot] = tmp[me.zat(d)]
    for e in range(XS):
        part0[:, e] = dot3(gbuf[0, :, me.cols(e)], q[0], 0).reshape(ZS, 16, RANK)
    own = scatter_plane(me, w, part0, part1, rb0, xb0, rb1, half1, whole1)
    gather_plane(me, w, own[0], own[1], full0, slots1, full1)
    for l in range(LAYERS):
        squares = jnp.zeros((1, RANK), F32)
        for e in range(XS):
            block = gathered(full0, full1, l, e)
            squares = squares + jnp.sum(block * block, 0, keepdims=True)
        sq[me.t, l] = jnp.broadcast_to(squares, (8, RANK))
    copies = [w.go(sq.at[me.t], sq.at[me.t], me.tdev(d)) for d in range(1, TP)]
    for l in range(LAYERS):
        for e in range(XS):
            block = gathered(full0, full1, l, e)
            new_mom[l, :, me.cols(e)] = gbuf[l, :, me.cols(e)] - (1.0 - keep_rate) * dot3(q[l], block, 1)
    for copy in copies:
        copy.wait_recv()
    for l in range(LAYERS):
        squares = sq[0, l]
        for t in range(1, TP):
            squares = squares + sq[t, l]
        norm = jnp.sqrt(squares[0:1] + eps)
        new_basis[l] = own[l] / norm
        scaled = q[l] * (math.sqrt(ROWS * COLS / RANK) / norm)
        for e in range(XS):
            update[l, :, me.cols(e)] = dot3(scaled, gathered(full0, full1, l, e), 1)
    w.drain()


def split3(a):
    high = a.astype(BF16)
    rest = a - high.astype(F32)
    mid = rest.astype(BF16)
    low = (rest - mid.astype(F32)).astype(BF16)
    return high, mid, low


def eliminate(a_ref, w_ref):
    b = 32
    lane = lax.broadcasted_iota(jnp.int32, (8, HALF), 1)
    row = lax.broadcasted_iota(jnp.int32, (8, HALF), 0)
    for r0 in range(0, RANK, b):
        groups = b // 8
        panel = [[a_ref[r0 + 8 * g : r0 + 8 * g + 8, h * HALF : (h + 1) * HALF] for h in (0, 1)] for g in range(groups)]
        for g0 in range(groups):
            side, start = divmod(r0 + 8 * g0, HALF)
            cols = {
                (k, g): jnp.broadcast_to(panel[g][side][:, start + k : start + k + 1], (8, HALF))
                for k in range(8) for g in range(g0, groups)
            }
            scale = jnp.zeros((8, HALF), F32)
            for k in range(8):
                pivot = jnp.broadcast_to(cols[k, g0][k : k + 1], (8, HALF))
                inverse = 1.0 / pivot
                scale = jnp.where(row == k, lax.rsqrt(pivot), scale)
                ratio = {g: cols[k, g] * inverse for g in range(g0, groups)}
                ratio[g0] = jnp.where(row > k, ratio[g0], 0.0)
                for n in range(k + 1, 8):
                    spread = jnp.broadcast_to(cols[n, g0][k : k + 1], (8, HALF))
                    for g in range(g0, groups):
                        cols[n, g] = cols[n, g] - ratio[g] * spread
                at = lane == start + k
                for h in (0, 1):
                    spread = jnp.broadcast_to(panel[g0][h][k : k + 1], (8, HALF))
                    if h == side:
                        spread = jnp.where(at, 1.0, spread)
                    for g in range(g0, groups):
                        kept = panel[g][h]
                        if h == side and g == g0:
                            kept = jnp.where(at & (row >= k), jnp.where(row == k, 1.0, 0.0), kept)
                        elif h == side:
                            kept = jnp.where(at, 0.0, kept)
                        panel[g][h] = kept - ratio[g] * spread
            for h in (0, 1):
                panel[g0][h] = panel[g0][h] * scale
        whole = jnp.concatenate([jnp.concatenate(panel[g], 1) for g in range(groups)], 0)
        lanes = lax.broadcasted_iota(jnp.int32, (b, RANK), 1)
        rows = lax.broadcasted_iota(jnp.int32, (b, RANK), 0) + r0
        w_ref[r0 : r0 + b, :] = jnp.where(lanes <= rows, whole, 0.0)
        rest = r0 + b
        if rest < RANK:
            right = jnp.where((lanes > rows) & (lanes < rest), 0.0, whole)
            h, m, l = split3(whole)
            hr, mr, lr = split3(right)
            left = jnp.concatenate([h, h, m, h, l, m], 0)
            base = rest // HALF * HALF
            change = lax.dot_general(
                left[:, base:], jnp.concatenate([hr, mr, hr, lr, hr, mr], 0),
                (((0,), (0,)), ((), ())), preferred_element_type=F32)
            wide = lax.broadcasted_iota(jnp.int32, (RANK - rest, RANK), 1)
            old = jnp.where((wide >= r0) & (wide < rest), 0.0, a_ref[rest:, :])
            a_ref[rest:, :] = old - change[rest - base :, :]


def factor_kernel(g, w_ref, a):
    a[...] = g[...]
    eliminate(a, w_ref)


def refine_kernel(g, w_ref, a):
    lanes = lax.broadcasted_iota(jnp.int32, (RANK, RANK), 1)
    rows = lax.broadcasted_iota(jnp.int32, (RANK, RANK), 0)
    unit = jnp.where(lanes == rows, 1.0, 0.0)

    def lower(e):
        return jnp.where(lanes < rows, e, jnp.where(lanes == rows, 0.5 * e, 0.0))

    start = g[...] - unit
    w_ref[...] = unit - lower(start)

    def more(state):
        size, step = state
        return (size > 1e-6) & (step < 6)

    def newton(state):
        inv = w_ref[...]
        error = dot(dot(inv, g[...], ((1,), (0,))), inv, ((1,), (1,))) - unit
        w_ref[...] = inv - dot(lower(error), inv, ((1,), (0,)))
        return jnp.sum(error * error), state[1] + 1

    size, _ = lax.while_loop(more, newton, (jnp.sum(start * start), 0))

    @pl.when(jnp.logical_not(size <= 1e-6))
    def _():
        a[...] = g[...]
        eliminate(a, w_ref)


def vmem(*shape):
    return pltpu.VMEM(shape, F32)


def params(collective_id):
    return pltpu.CompilerParams(collective_id=collective_id, has_side_effects=True, vmem_limit_bytes=60 * 2**20)


V = pl.BlockSpec(memory_space=pltpu.VMEM)
ANY = pl.BlockSpec(memory_space=pl.ANY)


def sums(n):
    return [
        vmem(2, RANK // 8, 8, HALF), vmem(2, RANK // 8, 8, HALF), vmem(ZS, 8, HALF), vmem(XS, 8, HALF),
        pltpu.SemaphoreType.DMA((n,)), pltpu.SemaphoreType.DMA((n,)),
    ]


def per_device(gradient, momentum, basis):
    rows, cols = gradient.shape[1:]
    share = basis.shape[1]
    small = jax.ShapeDtypeStruct((RANK, RANK), F32)
    tall = jax.ShapeDtypeStruct((rows, RANK), F32)
    product, gram = pl.pallas_call(
        first_kernel,
        out_shape=(tall, small),
        in_specs=[ANY, ANY, V],
        out_specs=(V, V),
        scratch_shapes=[
            vmem(LAYERS, rows, cols), vmem(LAYERS, rows, cols),
            vmem(ZS, XS, share, RANK), vmem(XS, ZS, share, RANK), vmem(XS, ZS, share, RANK),
            vmem(LAYERS, YS, rows // YS, RANK), vmem(TP, rows // YS, RANK),
        ] + sums(128) + [pltpu.SemaphoreType.DMA((2,))],
        compiler_params=params(0),
        name="first",
    )(gradient, momentum, basis)
    def factor(kernel, gram):
        return pl.pallas_call(
            kernel, out_shape=small, in_specs=[V], out_specs=V, scratch_shapes=[vmem(RANK, RANK)],
            compiler_params=pltpu.CompilerParams(vmem_limit_bytes=32 * 2**20), name="factor")(gram)

    inverse = factor(factor_kernel, gram)
    product, gram = pl.pallas_call(
        second_kernel,
        out_shape=(tall, small),
        in_specs=[V, V],
        out_specs=(V, V),
        scratch_shapes=sums(40),
        compiler_params=params(1),
        name="second",
    )(product, inverse)
    inverse = factor(refine_kernel, gram)
    whole = jax.ShapeDtypeStruct((LAYERS, rows, cols), F32)
    return pl.pallas_call(
        last_kernel,
        out_shape=(whole, jax.ShapeDtypeStruct((LAYERS, share, RANK), F32), whole),
        in_specs=[ANY, ANY, V, V],
        out_specs=(V, V, V),
        scratch_shapes=[
            vmem(LAYERS, rows, cols), vmem(LAYERS, rows, cols), vmem(LAYERS, rows, RANK),
            vmem(ZS, XS, share, RANK), vmem(XS, ZS, share, RANK), vmem(ZS, share, RANK),
            vmem(ZS, XS, share, RANK), vmem(XS, ZS, share, RANK), vmem(XS, ZS, share, RANK),
            vmem(2, 8, XS, share, RANK), vmem(XS, share, RANK), vmem(2, 8, share, RANK),
            vmem(ZS, share, RANK), vmem(2, ZS, share, RANK), vmem(TP, LAYERS, 8, RANK),
            pltpu.SemaphoreType.DMA((140,)), pltpu.SemaphoreType.DMA((140,)), pltpu.SemaphoreType.DMA((2,)),
        ],
        compiler_params=params(2),
        name="last",
    )(gradient, momentum, product, inverse)


def solution(mesh):
    return jax.shard_map(
        per_device,
        mesh=mesh,
        in_specs=(P(None, "fsdp", "tp"), P(None, "fsdp", "tp"), P(None, ("tp", "fsdp"), None)),
        out_specs=(P(None, "fsdp", "tp"), P(None, ("tp", "fsdp"), None), P(None, "fsdp", "tp")),
        check_vma=False,
    )
```

time: 260 us -> 225 us (0.87)
  Pallas kernels: 254 us -> 217 us
    pallas_call x2, Pallas kernels: 47 us -> 9.36 us  [factor(): pl.pallas_call(kernel, out_shape=small, in_specs=[V], out_specs=V, scratc...]
    pallas_call x1, Pallas kernels: 95.6 us -> 92.1 us  [per_device(): pl.pallas_call(last_kernel, out_shape=(whole, jax.ShapeDtypeStruct((LAYER...]
    pallas_call x1, Pallas kernels: 26.6 us -> 30.1 us  [per_device(): pl.pallas_call(second_kernel, out_shape=(tall, small), in_specs=[V, V], o...]
    unnamed x11 -> x15, local copies, waits for them, and re-layouts: 5.76 us -> 7.27 us
where the time goes in v2:
time: 225 us
  Pallas kernels  217 us (96%)
  local copies, waits for them, and re-layouts  7.27 us (3%)
    pallas_call x1, Pallas kernels, per_device(): pl.pallas_call(last_kernel, out_shape=(whole, jax.ShapeDtypeStruct((LAYER...  92.1 us
    pallas_call x1, Pallas kernels, per_device(): pl.pallas_call(first_kernel, out_shape=(tall, small), in_specs=[ANY, ANY,...  85 us
    pallas_call x1, Pallas kernels, per_device(): pl.pallas_call(second_kernel, out_shape=(tall, small), in_specs=[V, V], o...  30.1 us
    pallas_call x2, Pallas kernels, factor(): pl.pallas_call(kernel, out_shape=small, in_specs=[V], out_specs=V, scratc...  9.36 us
    unnamed x15, local copies, waits for them, and re-layouts  7.27 us

profile of v2, /device:TPU:1, one launch (start us, length us, event | category | flops | bytes accessed | tf_op | source)
XLA Modules:
  0.0 224.5 jit_solution(12215895465475519249)
XLA Ops:
  0.6 85.0 %first.1 = (f32[128,256]{1,0:T(8,128)}, f32[256,256]{1,0:T(8,128)}) custom-call(f32[2,128,1024]{2,1,0:T(8,128)} %grad.3, f32[2,128,1024]{2,1,0:T(8,128)} %mom.3, f32[2,16,256]{2,1,0:T(8,128)} %basis.1), custom_call_target="tpu_custom_call" | custom-call | tf_op jit(solution)/shard_map/first/pallas_call | solution.py:515
  85.7 0.0 copy-start.3
  85.7 0.9 copy-done.3
  86.6 7.6 %factor.2.inv = f32[256,256]{1,0:T(8,128)S(1)} custom-call(f32[256,256]{1,0:T(8,128)S(1)} %copy-done.3), custom_call_target="tpu_custom_call" | custom-call | tf_op jit(solution)/shard_map/factor/pallas_call | solution.py:529
  94.2 0.0 copy-start.1
  94.3 0.7 copy-done.1
  94.9 30.1 %second.1 = (f32[128,256]{1,0:T(8,128)}, f32[256,256]{1,0:T(8,128)}) custom-call(f32[128,256]{1,0:T(8,128)} %get-tuple-element.7.p, f32[256,256]{1,0:T(8,128)} %copy-done.1), custom_call_target="tpu_custom_call" | custom-call | tf_op jit(solution)/shard_map/second/pallas_call | solution.py:534
  125.0 0.0 copy-start.2
  125.0 0.9 copy-done.2
  126.0 1.8 factor.3.inv
  127.7 0.0 copy-start
  127.8 0.7 copy-done
  128.4 92.1 %last.1 = (f32[2,128,1024]{2,1,0:T(8,128)}, f32[2,16,256]{2,1,0:T(8,128)}, f32[2,128,1024]{2,1,0:T(8,128)}) custom-call(f32[2,128,1024]{2,1,0:T(8,128)} %grad.3, f32[2,128,1024]{2,1,0:T(8,128)} %mom.3, f32[128,256]{1,0:T(8,128)} %get-tuple-element.9.p, f32[256,256]{1,0:T(8,128)} %copy-done), custom_call_target="tpu_custom_call" | custom-call | tf_op jit(solution)/shard_map/last/pallas_call | solution.py:545
  220.5 0.0 copy-start.5
  220.5 0.0 copy-start.4
  220.5 2.4 %copy.9 = f32[2,128,1024]{2,1,0:T(8,128)} copy(f32[2,128,1024]{2,1,0:T(8,128)} %get-tuple-element.14) | data formatting | bytes 2097152
  222.9 0.0 copy-done.5
  222.9 0.6 copy.10
  223.6 0.0 copy-done.4
  223.6 1.0 copy.11
Async XLA Ops:
  85.7 1.0 copy-start.3
  94.2 0.7 copy-start.1
  125.0 1.0 copy-start.2
  127.7 0.7 copy-start
  220.5 2.4 %copy-start.5 = (f32[2,16,256]{2,1,0:T(8,128)S(1)}, f32[2,16,256]{2,1,0:T(8,128)}, u32[]{:S(2)}) copy-start(f32[2,16,256]{2,1,0:T(8,128)} %get-tuple-element.15) | copy-start | bytes 98308
  220.5 3.0 %copy-start.4 = (f32[2,128,1024]{2,1,0:T(8,128)S(1)}, f32[2,128,1024]{2,1,0:T(8,128)}, u32[]{:S(2)}) copy-start(f32[2,128,1024]{2,1,0:T(8,128)} %get-tuple-element.16) | copy-start | bytes 3145732

commit v3 on v2

v3 whole, which is shorter than its diff:
```python
import math

import jax
import jax.numpy as jnp
from jax import lax
from jax.experimental import pallas as pl
from jax.experimental.pallas import tpu as pltpu
from jax.sharding import PartitionSpec as P

ROWS = 8192
COLS = 8192
RANK = 256
LAYERS = 2
XS, ZS, YS, CS = 4, 16, 4, 2
TP = YS * CS
MESH = pl.DeviceIdType.MESH
HIGHEST = lax.Precision.HIGHEST
F32 = jnp.float32
BF16 = jnp.bfloat16
HALF = RANK // 2

keep_rate = 0.95
eps = 1e-06


def dot(a, b, dims):
    return lax.dot_general(a, b, (dims, ((), ())), precision=HIGHEST, preferred_element_type=F32)


def split2(a):
    high = a.astype(BF16)
    return high, (a - high.astype(F32)).astype(BF16)


def dot3(a, b, axis):
    ah, al = split2(a)
    bh, bl = split2(b)
    return lax.dot_general(
        jnp.concatenate([ah, ah, al], axis), jnp.concatenate([bh, bl, bh], axis),
        (((axis,), (axis,)), ((), ())), preferred_element_type=F32)


class Place:
    def __init__(self):
        self.f = lax.axis_index("fsdp")
        self.t = lax.axis_index("tp")
        self.x = lax.div(self.f, ZS)
        self.z = lax.rem(self.f, ZS)
        self.y = lax.div(self.t, CS)
        self.c = lax.rem(self.t, CS)

    def zat(self, d):
        return lax.rem(self.z + (ZS + d), ZS)

    def xat(self, d):
        return lax.rem(self.x + (XS + d), XS)

    def yat(self, d):
        return lax.rem(self.y + (YS + d), YS)

    def cols(self, e):
        return pl.ds(pl.multiple_of(self.xat(e) * 256, 256), 256)

    def zdev(self, d):
        return (self.x * ZS + self.zat(d), self.t)

    def xdev(self, d):
        return (self.xat(d) * ZS + self.z, self.t)

    def tdev(self, d):
        return (self.f, lax.rem(self.t + (TP + d), TP))

    def ydev(self, d):
        return (self.f, self.yat(d) * CS + self.c)

    def cdev(self):
        return (self.f, self.y * CS + (1 - self.c))


class Wires:
    def __init__(self, send, recv):
        self.send, self.recv, self.used = send, recv, 0
        self.sent = []

    def go(self, src, dst, device):
        i = self.used
        self.used += 1
        copy = pltpu.make_async_remote_copy(
            src_ref=src, dst_ref=dst, send_sem=self.send.at[i], recv_sem=self.recv.at[i],
            device_id=device, device_id_type=MESH,
        )
        copy.start()
        self.sent.append(copy)
        return copy

    def drain(self):
        for copy in self.sent:
            copy.wait_send()
        self.sent = []


def gathered(full0, full1, l, e):
    block = full0[:, e] if l == 0 else full1[e]
    return block.reshape(256, RANK)


def greet(devices):
    barrier = pltpu.get_barrier_semaphore()
    for device in devices:
        pl.semaphore_signal(barrier, inc=1, device_id=device, device_id_type=MESH)
    pl.semaphore_wait(barrier, len(devices))


WAYS = ((1, 8), (-1, 7))


def near(way, d):
    return 0 if d == 0 else 2 * d - 1 if way == 1 else 2 * d


def offset(slot):
    return 0 if slot == 0 else -((slot + 1) // 2) if slot % 2 else slot // 2


GROUPS = ((0, 5), (5, 9), (9, 13), (13, 16))


def gather_plane(me, w, own0, own1, full0, slots1, full1, beside):
    full0[me.z, 0] = own0
    slots1[0, 0] = own1
    full1[0, me.z] = own1
    xa = {e: w.go(full0.at[me.z, 0], full0.at[me.z, (-e) % XS], me.xdev(e)) for e in (3, 1, 2)}
    ring, wide, ahead = {}, {}, {}

    def hop_b(s):
        for way, last in WAYS:
            if 0 < s <= last:
                ring["b", way, s - 1].wait_recv()
            if s < last:
                ring["b", way, s] = w.go(
                    slots1.at[0, near(way, s)], slots1.at[0, near(way, s + 1)], me.zdev(way))

    def hop_a(s):
        for half in (0, 1):
            pair = pl.ds(2 * half, 2)
            for way, last in WAYS:
                if s == 0 and way == 1:
                    for e in ((3,), (1, 2))[half]:
                        xa[e].wait_recv()
                if 0 < s <= last:
                    ring["a", way, s - 1, half].wait_recv()
                if s < last:
                    block = full0.at[me.zat(-way * s), pair]
                    ring["a", way, s, half] = w.go(block, block, me.zdev(way))

    def spread(g):
        lo, hi = GROUPS[g]
        group = slots1.at[0, pl.ds(lo, hi - lo)]
        wide[g] = [w.go(group, slots1.at[(-e) % XS, pl.ds(lo, hi - lo)], me.xdev(e)) for e in (1, -1)]
        for i in range(lo, hi):
            full1[0, me.zat(offset(i))] = slots1[0, i]

    def forward(g):
        lo, hi = GROUPS[g]
        mid = (lo + hi) // 2
        ahead[g] = []
        for n, (a, b, e) in enumerate(((lo, mid, 1), (mid, hi, -1))):
            wide[g][n].wait_recv()
            ahead[g].append(
                w.go(slots1.at[(-e) % XS, pl.ds(a, b - a)], slots1.at[2, pl.ds(a, b - a)], me.xdev(e)))
        for i in range(lo, hi):
            for e in (1, 3):
                full1[e, me.zat(offset(i))] = slots1[e, i]

    for s in range(9):
        hop_b(s)
        if s in (2, 4, 6, 8):
            spread(s // 2 - 1)
        hop_a(s)
        if s in (4, 6, 8):
            forward(s // 2 - 2)
        beside(s)
    forward(3)
    for g in range(4):
        for copy in ahead[g]:
            copy.wait_recv()
        for i in range(*GROUPS[g]):
            full1[2, me.zat(offset(i))] = slots1[2, i]


FAR = [8] + [d for r in range(7, 0, -1) for d in (r, -r)] + [0]
FAR_GROUPS = ((0, 3), (3, 7), (7, 11), (11, 16))


def scatter_plane(me, w, part0, part1, rb0, xb0, rb1, half1, whole1, beside):
    first, second, ring = {}, {}, {}

    def begin(g):
        lo, hi = FAR_GROUPS[g]
        mid = (lo + hi) // 2
        first[g] = [
            w.go(part1.at[2, pl.ds(a, b - a)], half1.at[pl.ds(a, b - a)], me.xdev(e))
            for a, b, e in ((lo, mid, 1), (mid, hi, -1))
        ]

    def pass_on(g):
        lo, hi = FAR_GROUPS[g]
        mid = (lo + hi) // 2
        second[g] = []
        for n, (a, b, e) in enumerate(((lo, mid, 1), (mid, hi, -1))):
            first[g][n].wait_recv()
            part1[e % XS, a:b] = part1[e % XS, a:b] + half1[a:b]
            second[g].append(
                w.go(part1.at[e % XS, pl.ds(lo, hi - lo)], whole1.at[n, pl.ds(lo, hi - lo)], me.xdev(e)))

    def collect(g):
        lo, hi = FAR_GROUPS[g]
        for copy in second[g]:
            copy.wait_recv()
        part1[0, lo:hi] = part1[0, lo:hi] + whole1[0, lo:hi] + whole1[1, lo:hi]

    def hop_a(s):
        for half in (0, 1):
            lo, hi = 2 * half, 2 * half + 2
            pair = pl.ds(lo, 2)
            for k, (way, last) in enumerate(WAYS):
                if s > last:
                    continue
                there = me.zat(way * (last - s))
                if s == 0:
                    ring["a", way, 0, half] = w.go(part0.at[there, pair], rb0.at[k, 0, pair], me.zdev(way))
                    continue
                ring["a", way, s - 1, half].wait_recv()
                if s < last:
                    rb0[k, s - 1, lo:hi] = rb0[k, s - 1, lo:hi] + part0[there, lo:hi]
                    ring["a", way, s, half] = w.go(rb0.at[k, s - 1, pair], rb0.at[k, s, pair], me.zdev(way))

    def hop_b(s):
        for k, (way, last) in enumerate(WAYS):
            if s > last:
                continue
            slot = FAR.index(way * (last - s))
            if s == 0:
                ring["b", way, 0] = w.go(part1.at[0, slot], rb1.at[k, 0], me.zdev(way))
                continue
            ring["b", way, s - 1].wait_recv()
            if s < last:
                rb1[k, s - 1] = rb1[k, s - 1] + part1[0, slot]
                ring["b", way, s] = w.go(rb1.at[k, s - 1], rb1.at[k, s], me.zdev(way))

    for g in range(4):
        begin(g)
    copies = []
    for s in range(11):
        if s <= 8:
            hop_a(s)
        if s == 8:
            rb0[0, 7] = rb0[0, 7] + part0[me.z] + rb0[1, 6]
            copies = [w.go(rb0.at[0, 7, e], xb0.at[e], me.xdev(e)) for e in (2, 1, 3)]
        if s in (0, 2, 4, 6):
            pass_on(s // 2)
        if s in (1, 3, 5, 7):
            collect(s // 2)
        if s >= 2:
            hop_b(s - 2)
        beside(s)
    for copy in copies:
        copy.wait_recv()
    return rb0[0, 7, 0] + xb0[1] + xb0[2] + xb0[3], part1[0, 15] + rb1[0, 7] + rb1[1, 6]


def sum_gram(me, w, product, gs, gfull, zbuf, xbuf):
    gram = dot(product, product, ((0,), (0,)))
    for h in range(2):
        gs[h] = gram[:, h * HALF : (h + 1) * HALF].reshape(RANK // 8, 8, HALF)

    def tile(ref, z):
        return ref.at[lax.div(z, 8), me.y * 8 + lax.rem(z, 8)]

    far = [8] + [d for r in range(7, 0, -1) for d in (r, ZS - r)]
    copies = [w.go(tile(gs, me.zat(d)), zbuf.at[d], me.zdev(d)) for d in far]
    yield
    total = gs[lax.div(me.z, 8), me.y * 8 + lax.rem(me.z, 8)]
    for d, copy in reversed(list(zip(far, copies))):
        copy.wait_recv()
        total = total + zbuf[d]
    xbuf[me.x] = total
    copies = [w.go(xbuf.at[me.x], xbuf.at[me.x], me.xdev(d)) for d in (2, 1, 3)]
    yield
    for copy in copies:
        copy.wait_recv()
    gfull[lax.div(me.z, 8), me.y * 8 + lax.rem(me.z, 8)] = xbuf[0] + xbuf[1] + xbuf[2] + xbuf[3]
    copies = [w.go(tile(gfull, me.z), tile(gfull, me.z), me.zdev(d)) for d in far]
    yield
    for copy in reversed(copies):
        copy.wait_recv()
    mine = gfull.at[:, pl.ds(me.y * 8, 8)]
    copies = [w.go(mine, mine, me.ydev(d)) for d in (2, 1, 3)]
    yield
    for copy in copies:
        copy.wait_recv()


def kernel(grad, mom, basis, new_mom, new_basis, update,
           gbuf, mbuf, bfull0, bslots1, bfull1, part, rs, p, q, a, w1, w2,
           gs, gfull, zbuf, xbuf, gs2, gfull2, zbuf2, xbuf2,
           part0, part1, tmp, full0, slots1, full1, rb0, xb0, rb1, half1, whole1, sq,
           send, recv, local):
    me = Place()
    w = Wires(send, recv)
    loads = [pltpu.make_async_copy(grad, gbuf, local.at[0]), pltpu.make_async_copy(mom, mbuf, local.at[1])]
    for load in loads:
        load.start()
    greet([me.zdev(d) for d in range(1, ZS)] + [me.xdev(d) for d in range(1, XS)] + [me.tdev(d) for d in range(1, TP)])

    def load_buffer(s):
        if s == 0:
            for load in loads:
                load.wait()
            gbuf[...] = gbuf[...] + mbuf[...]

    gather_plane(me, w, basis[0], basis[1], bfull0, bslots1, bfull1, load_buffer)

    share = part.shape[2]
    for l in range(LAYERS):
        total = jnp.zeros((part.shape[1] * share, RANK), F32)
        for e in range(XS):
            total = total + dot(gbuf[l, :, me.cols(e)], gathered(bfull0, bfull1, l, e), ((1,), (0,)))
        part[l] = total.reshape(part.shape[1], share, RANK)
    copies = []
    for d in range(1, TP):
        there = lax.rem(me.t + d, TP)
        copies.append(w.go(part.at[lax.rem(there, CS), lax.div(there, CS)], rs.at[d], me.tdev(d)))
    total = part[me.c, me.y]
    for d in range(1, TP):
        copies[d - 1].wait_recv()
        total = total + rs[d]
    rows = pl.ds(me.y * share, share)
    p[rows] = total
    copies = [w.go(p.at[rows], p.at[rows], me.ydev(d)) for d in (2, 1, 3)]
    for copy in copies:
        copy.wait_recv()

    for _ in sum_gram(me, w, p[...], gs, gfull, zbuf, xbuf):
        pass
    for h in range(2):
        a[:, h * HALF : (h + 1) * HALF] = gfull[h].reshape(RANK, HALF)
    for r0 in range(0, RANK, PANEL):
        eliminate(a, w1, r0)
    q[me.c] = dot(p[...], w1[...], ((1,), (1,)))
    swap = w.go(q.at[me.c], q.at[me.c], me.cdev())

    second = sum_gram(me, w, q[me.c], gs2, gfull2, zbuf2, xbuf2)
    next(second)
    swap.wait_recv()
    for e in (2, 1, 3, 0):
        tmp[...] = dot3(gbuf[1, :, me.cols(e)], q[1], 0).reshape(ZS, 16, RANK)
        for slot, d in enumerate(FAR):
            part1[e, slot] = tmp[me.zat(d)]
    for e in range(XS):
        part0[:, e] = dot3(gbuf[0, :, me.cols(e)], q[0], 0).reshape(ZS, 16, RANK)

    def go_on(s):
        if s in (2, 4, 7, 10):
            next(second, None)

    own = scatter_plane(me, w, part0, part1, rb0, xb0, rb1, half1, whole1, go_on)
    for h in range(2):
        a[:, h * HALF : (h + 1) * HALF] = gfull2[h].reshape(RANK, HALF)
    trade = []

    def factor_on(s):
        if s < 8:
            eliminate(a, w2.at[me.c], s * PANEL)
        if s == 7:
            trade.append(w.go(w2.at[me.c], w2.at[me.c], me.cdev()))

    gather_plane(me, w, own[0], own[1], full0, slots1, full1, factor_on)
    trade[0].wait_recv()
    w.drain()
    for l in range(LAYERS):
        q[l] = dot(q[l], w2[l], ((1,), (1,)))
        squares = jnp.zeros((1, RANK), F32)
        for e in range(XS):
            block = dot3(gathered(full0, full1, l, e), w2[l], 1)
            if l == 0:
                part0[:, e] = block.reshape(ZS, 16, RANK)
            else:
                part1[e] = block.reshape(ZS, 16, RANK)
            squares = squares + jnp.sum(block * block, 0, keepdims=True)
        sq[me.t, l] = jnp.broadcast_to(squares, (8, RANK))
    copies = [w.go(sq.at[me.t], sq.at[me.t], me.tdev(d)) for d in range(1, TP)]
    for l in range(LAYERS):
        for e in range(XS):
            block = gathered(part0, part1, l, e)
            new_mom[l, :, me.cols(e)] = gbuf[l, :, me.cols(e)] - (1.0 - keep_rate) * dot3(q[l], block, 1)
    for copy in copies:
        copy.wait_recv()
    for l in range(LAYERS):
        squares = sq[0, l]
        for t in range(1, TP):
            squares = squares + sq[t, l]
        norm = jnp.sqrt(squares[0:1] + eps)
        new_basis[l] = (part0[me.z, 0] if l == 0 else part1[0, me.z]) / norm
        scaled = q[l] * (math.sqrt(ROWS * COLS / RANK) / norm)
        for e in range(XS):
            update[l, :, me.cols(e)] = dot3(scaled, gathered(part0, part1, l, e), 1)
    w.drain()


PANEL = 32


def split3(a):
    high = a.astype(BF16)
    rest = a - high.astype(F32)
    mid = rest.astype(BF16)
    low = (rest - mid.astype(F32)).astype(BF16)
    return high, mid, low


def eliminate(a_ref, w_ref, r0):
    halves = [a_ref[r0 : r0 + PANEL, h * HALF : (h + 1) * HALF] for h in (0, 1)]
    finished = []
    for j0 in range(r0, r0 + PANEL, 8):
        side, start = divmod(j0, HALF)
        height = r0 + PANEL - j0
        lane = lax.broadcasted_iota(jnp.int32, (height, HALF), 1)
        row = lax.broadcasted_iota(jnp.int32, (height, HALF), 0)
        cols = [jnp.broadcast_to(halves[side][:, start + k : start + k + 1], (height, HALF)) for k in range(8)]
        scale = jnp.zeros((8, HALF), F32)
        for k in range(8):
            pivot = cols[k][k : k + 1]
            ratio = jnp.where(row > k, cols[k] * (1.0 / pivot), 0.0)
            scale = jnp.where(row[:8] == k, lax.rsqrt(pivot), scale)
            for n in range(k + 1, 8):
                cols[n] = cols[n] - ratio * cols[n][k : k + 1]
            for h in (0, 1):
                kept, spread = halves[h], halves[h][k : k + 1]
                if h == side:
                    spread = jnp.where(lane[0:1] == start + k, 1.0, spread)
                    kept = jnp.where((lane == start + k) & (row >= k), jnp.where(row == k, 1.0, 0.0), kept)
                halves[h] = kept - ratio * spread
        finished.append([half[:8] * scale for half in halves])
        halves = [half[8:] for half in halves] if height > 8 else None
    whole = jnp.concatenate([jnp.concatenate(rows, 1) for rows in finished], 0)
    lanes = lax.broadcasted_iota(jnp.int32, (PANEL, RANK), 1)
    rows = lax.broadcasted_iota(jnp.int32, (PANEL, RANK), 0) + r0
    w_ref[r0 : r0 + PANEL, :] = jnp.where(lanes <= rows, whole, 0.0)
    rest = r0 + PANEL
    if rest < RANK:
        right = jnp.where((lanes > rows) & (lanes < rest), 0.0, whole)
        h, m, l = split3(whole)
        hr, mr, lr = split3(right)
        left = jnp.concatenate([h, h, m, h, l, m], 0)
        base = rest // HALF * HALF
        change = lax.dot_general(
            left[:, base:], jnp.concatenate([hr, mr, hr, lr, hr, mr], 0),
            (((0,), (0,)), ((), ())), preferred_element_type=F32)
        wide = lax.broadcasted_iota(jnp.int32, (RANK - rest, RANK), 1)
        old = jnp.where((wide >= r0) & (wide < rest), 0.0, a_ref[rest:, :])
        a_ref[rest:, :] = old - change[rest - base :, :]


def vmem(*shape):
    return pltpu.VMEM(shape, F32)


V = pl.BlockSpec(memory_space=pltpu.VMEM)
ANY = pl.BlockSpec(memory_space=pl.ANY)
COPIES = 288


def per_device(gradient, momentum, basis):
    rows, cols = gradient.shape[1:]
    share = basis.shape[1]
    whole = jax.ShapeDtypeStruct((LAYERS, rows, cols), F32)
    plane = [vmem(ZS, XS, share, RANK), vmem(XS, ZS, share, RANK), vmem(XS, ZS, share, RANK)]
    sums = [vmem(2, RANK // 8, 8, HALF), vmem(2, RANK // 8, 8, HALF), vmem(ZS, 8, HALF), vmem(XS, 8, HALF)]
    return pl.pallas_call(
        kernel,
        out_shape=(whole, jax.ShapeDtypeStruct((LAYERS, share, RANK), F32), whole),
        in_specs=[ANY, ANY, V],
        out_specs=(V, V, V),
        scratch_shapes=[
            vmem(LAYERS, rows, cols), vmem(LAYERS, rows, cols), *plane,
            vmem(LAYERS, YS, rows // YS, RANK), vmem(TP, rows // YS, RANK), vmem(rows, RANK),
            vmem(LAYERS, rows, RANK), vmem(RANK, RANK), vmem(RANK, RANK), vmem(LAYERS, RANK, RANK),
            *sums, *sums,
            vmem(ZS, XS, share, RANK), vmem(XS, ZS, share, RANK), vmem(ZS, share, RANK), *plane,
            vmem(2, 8, XS, share, RANK), vmem(XS, share, RANK), vmem(2, 8, share, RANK),
            vmem(ZS, share, RANK), vmem(2, ZS, share, RANK), vmem(TP, LAYERS, 8, RANK),
            pltpu.SemaphoreType.DMA((COPIES,)), pltpu.SemaphoreType.DMA((COPIES,)), pltpu.SemaphoreType.DMA((2,)),
        ],
        compiler_params=pltpu.CompilerParams(
            collective_id=0, has_side_effects=True, vmem_limit_bytes=60 * 2**20),
        name="step",
    )(gradient, momentum, basis)


def solution(mesh):
    return jax.shard_map(
        per_device,
        mesh=mesh,
        in_specs=(P(None, "fsdp", "tp"), P(None, "fsdp", "tp"), P(None, ("tp", "fsdp"), None)),
        out_specs=(P(None, "fsdp", "tp"), P(None, ("tp", "fsdp"), None), P(None, "fsdp", "tp")),
        check_vma=False,
    )
```

time: 225 us -> 182 us (0.81)
  Pallas kernels: 217 us -> 177 us
  local copies, waits for them, and re-layouts: 7.27 us -> 3.99 us
    pallas_call x5 -> x1, Pallas kernels: 217 us -> 177 us  [per_device(): pl.pallas_call(kernel, out_shape=(whole, jax.ShapeDtypeStruct((LAYERS, sh...]
    unnamed x15 -> x7, local copies, waits for them, and re-layouts: 7.27 us -> 3.99 us
where the time goes in v3:
time: 182 us; the launch traced here: 181 us
  Pallas kernels  177 us (97%)
  local copies, waits for them, and re-layouts  3.99 us (2%)
    pallas_call x1, Pallas kernels, per_device(): pl.pallas_call(kernel, out_shape=(whole, jax.ShapeDtypeStruct((LAYERS, sh...  177 us
    unnamed x7, local copies, waits for them, and re-layouts  3.99 us

profile of v3, /device:TPU:1, one launch (start us, length us, event | category | flops | bytes accessed | tf_op | source)
XLA Modules:
  0.0 181.4 jit_solution(11458016474453448442)
XLA Ops:
  0.6 176.8 %step.1 = (f32[2,128,1024]{2,1,0:T(8,128)}, f32[2,16,256]{2,1,0:T(8,128)}, f32[2,128,1024]{2,1,0:T(8,128)}) custom-call(f32[2,128,1024]{2,1,0:T(8,128)} %grad.1, f32[2,128,1024]{2,1,0:T(8,128)} %mom.1, f32[2,16,256]{2,1,0:T(8,128)} %basis.1), custom_call_target="tpu_custom_call" | custom-call | tf_op jit(solution)/shard_map/step/pallas_call | solution.py:480
  177.4 0.0 copy-start.1
  177.4 0.0 copy-start
  177.4 2.4 %copy.9 = f32[2,128,1024]{2,1,0:T(8,128)} copy(f32[2,128,1024]{2,1,0:T(8,128)} %get-tuple-element.6) | data formatting | bytes 2097152
  179.8 0.0 copy-done.1
  179.8 0.6 copy.10
  180.5 0.0 copy-done
  180.5 1.0 copy.11
Async XLA Ops:
  177.4 2.4 %copy-start.1 = (f32[2,16,256]{2,1,0:T(8,128)S(1)}, f32[2,16,256]{2,1,0:T(8,128)}, u32[]{:S(2)}) copy-start(f32[2,16,256]{2,1,0:T(8,128)} %get-tuple-element.7) | copy-start | bytes 98308
  177.4 3.0 %copy-start = (f32[2,128,1024]{2,1,0:T(8,128)S(1)}, f32[2,128,1024]{2,1,0:T(8,128)}, u32[]{:S(2)}) copy-start(f32[2,128,1024]{2,1,0:T(8,128)} %get-tuple-element.8) | copy-start | bytes 3145732

commit v4 on v3

--- a/solution.py
+++ b/solution.py
@@ -192,7 +192,7 @@
 FAR_GROUPS = ((0, 3), (3, 7), (7, 11), (11, 16))
 
 
-def scatter_plane(me, w, part0, part1, rb0, xb0, rb1, half1, whole1, beside):
+def scatter_plane(me, w, part0, part1, rb0, xb0, rb1, half1, whole1, fill0, fill1, beside):
     first, second, ring = {}, {}, {}
 
     def begin(g):
@@ -248,12 +248,19 @@
                 rb1[k, s - 1] = rb1[k, s - 1] + part1[0, slot]
                 ring["b", way, s] = w.go(rb1.at[k, s - 1], rb1.at[k, s], me.zdev(way))
 
+    fill1(2)
     for g in range(4):
         begin(g)
+    fill0()
     copies = []
     for s in range(11):
         if s <= 8:
             hop_a(s)
+        if s == 0:
+            fill1(1)
+            fill1(3)
+        if s == 1:
+            fill1(0)
         if s == 8:
             rb0[0, 7] = rb0[0, 7] + part0[me.z] + rb0[1, 6]
             copies = [w.go(rb0.at[0, 7, e], xb0.at[e], me.xdev(e)) for e in (2, 1, 3)]
@@ -302,9 +309,9 @@
 
 
 def kernel(grad, mom, basis, new_mom, new_basis, update,
-           gbuf, mbuf, bfull0, bslots1, bfull1, part, rs, p, q, a, w1, w2,
+           gbuf, mbuf, bfull0, bslots1, bfull1, part, rs, q, p1, p2, a, w1, w2, wide,
            gs, gfull, zbuf, xbuf, gs2, gfull2, zbuf2, xbuf2,
-           part0, part1, tmp, full0, slots1, full1, rb0, xb0, rb1, half1, whole1, sq,
+           part0, part1, tmp, full0, slots1, full1, rb0, xb0, rb1, half1, whole1, cols0, cols1, sq,
            send, recv, local):
     me = Place()
     w = Wires(send, recv)
@@ -335,65 +342,74 @@
     for d in range(1, TP):
         copies[d - 1].wait_recv()
         total = total + rs[d]
-    rows = pl.ds(me.y * share, share)
-    p[rows] = total
-    copies = [w.go(p.at[rows], p.at[rows], me.ydev(d)) for d in (2, 1, 3)]
+    q[me.c, me.y] = total
+    copies = [w.go(q.at[me.c, me.y], q.at[me.c, me.y], me.tdev(d)) for d in range(1, TP)]
     for copy in copies:
         copy.wait_recv()
 
-    for _ in sum_gram(me, w, p[...], gs, gfull, zbuf, xbuf):
-        pass
-    for h in range(2):
-        a[:, h * HALF : (h + 1) * HALF] = gfull[h].reshape(RANK, HALF)
-    for r0 in range(0, RANK, PANEL):
-        eliminate(a, w1, r0)
-    q[me.c] = dot(p[...], w1[...], ((1,), (1,)))
-    swap = w.go(q.at[me.c], q.at[me.c], me.cdev())
-
-    second = sum_gram(me, w, q[me.c], gs2, gfull2, zbuf2, xbuf2)
-    next(second)
-    swap.wait_recv()
-    for e in (2, 1, 3, 0):
-        tmp[...] = dot3(gbuf[1, :, me.cols(e)], q[1], 0).reshape(ZS, 16, RANK)
+    def take(gram):
+        for h in range(2):
+            a[:, h * HALF : (h + 1) * HALF] = gram[h].reshape(RANK, HALF)
+
+    sums = [sum_gram(me, w, q[me.c].reshape(YS * share, RANK), gs, gfull, zbuf, xbuf)]
+    next(sums[0])
+    trade = []
+
+    def fill0():
+        for e in range(XS):
+            cols = dot(gbuf[0, :, me.cols(e)], q[0].reshape(YS * share, RANK), ((0,), (0,)))
+            part0[:, e] = cols.reshape(ZS, 16, RANK)
+
+    def fill1(e):
+        cols = dot(gbuf[1, :, me.cols(e)], q[1].reshape(YS * share, RANK), ((0,), (0,)))
+        tmp[...] = cols.reshape(ZS, 16, RANK)
         for slot, d in enumerate(FAR):
             part1[e, slot] = tmp[me.zat(d)]
-    for e in range(XS):
-        part0[:, e] = dot3(gbuf[0, :, me.cols(e)], q[0], 0).reshape(ZS, 16, RANK)
-
-    def go_on(s):
-        if s in (2, 4, 7, 10):
-            next(second, None)
-
-    own = scatter_plane(me, w, part0, part1, rb0, xb0, rb1, half1, whole1, go_on)
-    for h in range(2):
-        a[:, h * HALF : (h + 1) * HALF] = gfull2[h].reshape(RANK, HALF)
-    trade = []
-
-    def factor_on(s):
-        if s < 8:
-            eliminate(a, w2.at[me.c], s * PANEL)
-        if s == 7:
-            trade.append(w.go(w2.at[me.c], w2.at[me.c], me.cdev()))
-
-    gather_plane(me, w, own[0], own[1], full0, slots1, full1, factor_on)
-    trade[0].wait_recv()
-    w.drain()
+
+    def beside_scatter(s):
+        if s in (1, 2, 4, 6):
+            next(sums[0], None)
+        if s == 6:
+            take(gfull)
+        for n in {7: (0, 1, 2), 8: (3, 4, 5), 9: (6, 7)}.get(s, ()):
+            eliminate(a, w1, n * PANEL)
+        if s == 9:
+            p1[...] = dot(q[me.c].reshape(YS * share, RANK), w1[...], ((1,), (1,)))
+            sums.append(sum_gram(me, w, p1[...], gs2, gfull2, zbuf2, xbuf2))
+            next(sums[1])
+
+    def beside_gather(s):
+        if s in (0, 1, 3, 5):
+            next(sums[1], None)
+        if s == 5:
+            take(gfull2)
+        for n in {5: (0,), 6: (1, 2, 3), 7: (4, 5, 6), 8: (7,)}.get(s, ()):
+            eliminate(a, w2, n * PANEL)
+        if s == 8:
+            wide[me.c] = dot(w2[...], w1[...], ((1,), (0,)))
+            trade.append(w.go(wide.at[me.c], wide.at[me.c], me.cdev()))
+            p2[me.c] = dot(p1[...], w2[...], ((1,), (1,)))
+            trade.append(w.go(p2.at[me.c], p2.at[me.c], me.cdev()))
+
+    own = scatter_plane(me, w, part0, part1, rb0, xb0, rb1, half1, whole1, fill0, fill1, beside_scatter)
+    gather_plane(me, w, own[0], own[1], full0, slots1, full1, beside_gather)
+    for copy in trade:
+        copy.wait_recv()
     for l in range(LAYERS):
-        q[l] = dot(q[l], w2[l], ((1,), (1,)))
         squares = jnp.zeros((1, RANK), F32)
         for e in range(XS):
-            block = dot3(gathered(full0, full1, l, e), w2[l], 1)
+            block = dot(gathered(full0, full1, l, e), wide[l], ((1,), (1,)))
             if l == 0:
-                part0[:, e] = block.reshape(ZS, 16, RANK)
+                cols0[:, e] = block.reshape(ZS, 16, RANK)
             else:
-                part1[e] = block.reshape(ZS, 16, RANK)
+                cols1[e] = block.reshape(ZS, 16, RANK)
             squares = squares + jnp.sum(block * block, 0, keepdims=True)
         sq[me.t, l] = jnp.broadcast_to(squares, (8, RANK))
     copies = [w.go(sq.at[me.t], sq.at[me.t], me.tdev(d)) for d in range(1, TP)]
     for l in range(LAYERS):
         for e in range(XS):
-            block = gathered(part0, part1, l, e)
-            new_mom[l, :, me.cols(e)] = gbuf[l, :, me.cols(e)] - (1.0 - keep_rate) * dot3(q[l], block, 1)
+            block = gathered(cols0, cols1, l, e)
+            new_mom[l, :, me.cols(e)] = gbuf[l, :, me.cols(e)] - (1.0 - keep_rate) * dot3(p2[l], block, 1)
     for copy in copies:
         copy.wait_recv()
     for l in range(LAYERS):
@@ -401,10 +417,10 @@
         for t in range(1, TP):
             squares = squares + sq[t, l]
         norm = jnp.sqrt(squares[0:1] + eps)
-        new_basis[l] = (part0[me.z, 0] if l == 0 else part1[0, me.z]) / norm
-        scaled = q[l] * (math.sqrt(ROWS * COLS / RANK) / norm)
+        new_basis[l] = (cols0[me.z, 0] if l == 0 else cols1[0, me.z]) / norm
+        scaled = p2[l] * (math.sqrt(ROWS * COLS / RANK) / norm)
         for e in range(XS):
-            update[l, :, me.cols(e)] = dot3(scaled, gathered(part0, part1, l, e), 1)
+            update[l, :, me.cols(e)] = dot3(scaled, gathered(cols0, cols1, l, e), 1)
     w.drain()
 
 
@@ -484,12 +500,14 @@
         out_specs=(V, V, V),
         scratch_shapes=[
             vmem(LAYERS, rows, cols), vmem(LAYERS, rows, cols), *plane,
-            vmem(LAYERS, YS, rows // YS, RANK), vmem(TP, rows // YS, RANK), vmem(rows, RANK),
-            vmem(LAYERS, rows, RANK), vmem(RANK, RANK), vmem(RANK, RANK), vmem(LAYERS, RANK, RANK),
+            vmem(LAYERS, YS, rows // YS, RANK), vmem(TP, rows // YS, RANK), vmem(LAYERS, YS, rows // YS, RANK),
+            vmem(rows, RANK), vmem(LAYERS, rows, RANK),
+            vmem(RANK, RANK), vmem(RANK, RANK), vmem(RANK, RANK), vmem(LAYERS, RANK, RANK),
             *sums, *sums,
             vmem(ZS, XS, share, RANK), vmem(XS, ZS, share, RANK), vmem(ZS, share, RANK), *plane,
             vmem(2, 8, XS, share, RANK), vmem(XS, share, RANK), vmem(2, 8, share, RANK),
-            vmem(ZS, share, RANK), vmem(2, ZS, share, RANK), vmem(TP, LAYERS, 8, RANK),
+            vmem(ZS, share, RANK), vmem(2, ZS, share, RANK),
+            vmem(ZS, XS, share, RANK), vmem(XS, ZS, share, RANK), vmem(TP, LAYERS, 8, RANK),
             pltpu.SemaphoreType.DMA((COPIES,)), pltpu.SemaphoreType.DMA((COPIES,)), pltpu.SemaphoreType.DMA((2,)),
         ],
         compiler_params=pltpu.CompilerParams(

time: 182 us -> 165 us (0.907)
  Pallas kernels: 177 us -> 160 us
    pallas_call x1, Pallas kernels: 177 us -> 160 us  [per_device(): pl.pallas_call(kernel, out_shape=(whole, jax.ShapeDtypeStruct((LAYERS, sh...]
where the time goes in v4:
time: 165 us
  Pallas kernels  160 us (97%)
  local copies, waits for them, and re-layouts  3.99 us (2%)
    pallas_call x1, Pallas kernels, per_device(): pl.pallas_call(kernel, out_shape=(whole, jax.ShapeDtypeStruct((LAYERS, sh...  160 us
    unnamed x7, local copies, waits for them, and re-layouts  3.99 us

profile of v4, /device:TPU:1, one launch (start us, length us, event | category | flops | bytes accessed | tf_op | source)
XLA Modules:
  0.0 164.9 jit_solution(10584460779666170604)
XLA Ops:
  0.6 160.3 %step.1 = (f32[2,128,1024]{2,1,0:T(8,128)}, f32[2,16,256]{2,1,0:T(8,128)}, f32[2,128,1024]{2,1,0:T(8,128)}) custom-call(f32[2,128,1024]{2,1,0:T(8,128)} %grad.1, f32[2,128,1024]{2,1,0:T(8,128)} %mom.1, f32[2,16,256]{2,1,0:T(8,128)} %basis.1), custom_call_target="tpu_custom_call" | custom-call | tf_op jit(solution)/shard_map/step/pallas_call | solution.py:496
  160.9 0.0 copy-start.1
  160.9 0.0 copy-start
  161.0 2.4 %copy.9 = f32[2,128,1024]{2,1,0:T(8,128)} copy(f32[2,128,1024]{2,1,0:T(8,128)} %get-tuple-element.6) | data formatting | bytes 2097152
  163.4 0.0 copy-done.1
  163.4 0.6 copy.10
  164.0 0.0 copy-done
  164.0 1.0 copy.11
Async XLA Ops:
  160.9 2.4 %copy-start.1 = (f32[2,16,256]{2,1,0:T(8,128)S(1)}, f32[2,16,256]{2,1,0:T(8,128)}, u32[]{:S(2)}) copy-start(f32[2,16,256]{2,1,0:T(8,128)} %get-tuple-element.7) | copy-start | bytes 98308
  160.9 3.0 %copy-start = (f32[2,128,1024]{2,1,0:T(8,128)S(1)}, f32[2,128,1024]{2,1,0:T(8,128)}, u32[]{:S(2)}) copy-start(f32[2,128,1024]{2,1,0:T(8,128)} %get-tuple-element.8) | copy-start | bytes 3145732

commit v5 on v4

--- a/solution.py
+++ b/solution.py
@@ -93,10 +93,9 @@
         self.sent.append(copy)
         return copy
 
-    def drain(self):
-        for copy in self.sent:
-            copy.wait_send()
-        self.sent = []
+    def drain(self, keep=0):
+        while len(self.sent) > keep:
+            self.sent.pop(0).wait_send()
 
 
 def gathered(full0, full1, l, e):
@@ -180,7 +179,9 @@
         if s in (4, 6, 8):
             forward(s // 2 - 2)
         beside(s)
+        w.drain(64)
     forward(3)
+    beside(9)
     for g in range(4):
         for copy in ahead[g]:
             copy.wait_recv()
@@ -271,23 +272,27 @@
         if s >= 2:
             hop_b(s - 2)
         beside(s)
+        w.drain(64)
     for copy in copies:
         copy.wait_recv()
     return rb0[0, 7, 0] + xb0[1] + xb0[2] + xb0[3], part1[0, 15] + rb1[0, 7] + rb1[1, 6]
+
+
+QUARTERS = ((0, 0), (0, 1), (1, 1), (1, 0))
 
 
 def sum_gram(me, w, product, gs, gfull, zbuf, xbuf):
     gram = dot(product, product, ((0,), (0,)))
-    for h in range(2):
-        gs[h] = gram[:, h * HALF : (h + 1) * HALF].reshape(RANK // 8, 8, HALF)
+    for n, (r, h) in enumerate(QUARTERS):
+        gs[n] = gram[r * HALF : (r + 1) * HALF, h * HALF : (h + 1) * HALF].reshape(HALF // 8, 8, HALF)
 
     def tile(ref, z):
-        return ref.at[lax.div(z, 8), me.y * 8 + lax.rem(z, 8)]
+        return ref.at[lax.div(z, 4), me.y * 4 + lax.rem(z, 4)]
 
     far = [8] + [d for r in range(7, 0, -1) for d in (r, ZS - r)]
     copies = [w.go(tile(gs, me.zat(d)), zbuf.at[d], me.zdev(d)) for d in far]
     yield
-    total = gs[lax.div(me.z, 8), me.y * 8 + lax.rem(me.z, 8)]
+    total = gs[lax.div(me.z, 4), me.y * 4 + lax.rem(me.z, 4)]
     for d, copy in reversed(list(zip(far, copies))):
         copy.wait_recv()
         total = total + zbuf[d]
@@ -296,12 +301,12 @@
     yield
     for copy in copies:
         copy.wait_recv()
-    gfull[lax.div(me.z, 8), me.y * 8 + lax.rem(me.z, 8)] = xbuf[0] + xbuf[1] + xbuf[2] + xbuf[3]
+    gfull[lax.div(me.z, 4), me.y * 4 + lax.rem(me.z, 4)] = xbuf[0] + xbuf[1] + xbuf[2] + xbuf[3]
     copies = [w.go(tile(gfull, me.z), tile(gfull, me.z), me.zdev(d)) for d in far]
     yield
     for copy in reversed(copies):
         copy.wait_recv()
-    mine = gfull.at[:, pl.ds(me.y * 8, 8)]
+    mine = gfull.at[pl.ds(0, 3), pl.ds(me.y * 4, 4)]
     copies = [w.go(mine, mine, me.ydev(d)) for d in (2, 1, 3)]
     yield
     for copy in copies:
@@ -311,7 +316,7 @@
 def kernel(grad, mom, basis, new_mom, new_basis, update,
            gbuf, mbuf, bfull0, bslots1, bfull1, part, rs, q, p1, p2, a, w1, w2, wide,
            gs, gfull, zbuf, xbuf, gs2, gfull2, zbuf2, xbuf2,
-           part0, part1, tmp, full0, slots1, full1, rb0, xb0, rb1, half1, whole1, cols0, cols1, sq,
+           part0, part1, tmp, full0, slots1, full1, rb0, xb0, rb1, half1, whole1, cols0, cols1, sq, out,
            send, recv, local):
     me = Place()
     w = Wires(send, recv)
@@ -320,39 +325,47 @@
         load.start()
     greet([me.zdev(d) for d in range(1, ZS)] + [me.xdev(d) for d in range(1, XS)] + [me.tdev(d) for d in range(1, TP)])
 
-    def load_buffer(s):
+    share = part.shape[2]
+
+    def multiply(l):
+        total = jnp.zeros((part.shape[1] * share, RANK), F32)
+        for e in range(XS):
+            total = total + dot(gbuf[l, :, me.cols(e)], gathered(bfull0, bfull1, l, e), ((1,), (0,)))
+        part[l] = total.reshape(part.shape[1], share, RANK)
+
+    def beside_basis(s):
         if s == 0:
             for load in loads:
                 load.wait()
             gbuf[...] = gbuf[...] + mbuf[...]
-
-    gather_plane(me, w, basis[0], basis[1], bfull0, bslots1, bfull1, load_buffer)
-
-    share = part.shape[2]
-    for l in range(LAYERS):
-        total = jnp.zeros((part.shape[1] * share, RANK), F32)
-        for e in range(XS):
-            total = total + dot(gbuf[l, :, me.cols(e)], gathered(bfull0, bfull1, l, e), ((1,), (0,)))
-        part[l] = total.reshape(part.shape[1], share, RANK)
+        if s == 9:
+            multiply(0)
+
+    gather_plane(me, w, basis[0], basis[1], bfull0, bslots1, bfull1, beside_basis)
+    multiply(1)
     copies = []
-    for d in range(1, TP):
+    away = (4, 3, 5, 2, 6, 1, 7)
+    for d in away:
         there = lax.rem(me.t + d, TP)
         copies.append(w.go(part.at[lax.rem(there, CS), lax.div(there, CS)], rs.at[d], me.tdev(d)))
     total = part[me.c, me.y]
-    for d in range(1, TP):
-        copies[d - 1].wait_recv()
+    for d, copy in zip(away, copies):
+        copy.wait_recv()
         total = total + rs[d]
     q[me.c, me.y] = total
-    copies = [w.go(q.at[me.c, me.y], q.at[me.c, me.y], me.tdev(d)) for d in range(1, TP)]
-    for copy in copies:
-        copy.wait_recv()
+    copies = [w.go(q.at[me.c, me.y], q.at[me.c, me.y], me.ydev(d)) for d in (2, 1, 3)]
+    for copy in copies:
+        copy.wait_recv()
+    swap = w.go(q.at[me.c], q.at[me.c], me.cdev())
 
     def take(gram):
-        for h in range(2):
-            a[:, h * HALF : (h + 1) * HALF] = gram[h].reshape(RANK, HALF)
+        for n, (r, h) in enumerate(QUARTERS):
+            quarter = gram[n].reshape(HALF, HALF) if n < 3 else jnp.zeros((HALF, HALF), F32)
+            a[r * HALF : (r + 1) * HALF, h * HALF : (h + 1) * HALF] = quarter
 
     sums = [sum_gram(me, w, q[me.c].reshape(YS * share, RANK), gs, gfull, zbuf, xbuf)]
     next(sums[0])
+    swap.wait_recv()
     trade = []
 
     def fill0():
@@ -385,17 +398,17 @@
             take(gfull2)
         for n in {5: (0,), 6: (1, 2, 3), 7: (4, 5, 6), 8: (7,)}.get(s, ()):
             eliminate(a, w2, n * PANEL)
+        if s == 9:
+            for copy in trade:
+                copy.wait_recv()
+            finish(0)
         if s == 8:
             wide[me.c] = dot(w2[...], w1[...], ((1,), (0,)))
             trade.append(w.go(wide.at[me.c], wide.at[me.c], me.cdev()))
             p2[me.c] = dot(p1[...], w2[...], ((1,), (1,)))
             trade.append(w.go(p2.at[me.c], p2.at[me.c], me.cdev()))
 
-    own = scatter_plane(me, w, part0, part1, rb0, xb0, rb1, half1, whole1, fill0, fill1, beside_scatter)
-    gather_plane(me, w, own[0], own[1], full0, slots1, full1, beside_gather)
-    for copy in trade:
-        copy.wait_recv()
-    for l in range(LAYERS):
+    def finish(l):
         squares = jnp.zeros((1, RANK), F32)
         for e in range(XS):
             block = dot(gathered(full0, full1, l, e), wide[l], ((1,), (1,)))
@@ -405,11 +418,18 @@
                 cols1[e] = block.reshape(ZS, 16, RANK)
             squares = squares + jnp.sum(block * block, 0, keepdims=True)
         sq[me.t, l] = jnp.broadcast_to(squares, (8, RANK))
+
+    own = scatter_plane(me, w, part0, part1, rb0, xb0, rb1, half1, whole1, fill0, fill1, beside_scatter)
+    gather_plane(me, w, own[0], own[1], full0, slots1, full1, beside_gather)
+    finish(1)
+    stores = []
     copies = [w.go(sq.at[me.t], sq.at[me.t], me.tdev(d)) for d in range(1, TP)]
     for l in range(LAYERS):
         for e in range(XS):
             block = gathered(cols0, cols1, l, e)
-            new_mom[l, :, me.cols(e)] = gbuf[l, :, me.cols(e)] - (1.0 - keep_rate) * dot3(p2[l], block, 1)
+            mbuf[l, :, me.cols(e)] = gbuf[l, :, me.cols(e)] - (1.0 - keep_rate) * dot3(p2[l], block, 1)
+        stores.append(pltpu.make_async_copy(mbuf.at[l], new_mom.at[l], local.at[2 + l]))
+        stores[-1].start()
     for copy in copies:
         copy.wait_recv()
     for l in range(LAYERS):
@@ -420,8 +440,12 @@
         new_basis[l] = (cols0[me.z, 0] if l == 0 else cols1[0, me.z]) / norm
         scaled = p2[l] * (math.sqrt(ROWS * COLS / RANK) / norm)
         for e in range(XS):
-            update[l, :, me.cols(e)] = dot3(scaled, gathered(cols0, cols1, l, e), 1)
+            out[l, :, me.cols(e)] = dot3(scaled, gathered(cols0, cols1, l, e), 1)
+        stores.append(pltpu.make_async_copy(out.at[l], update.at[l], local.at[4 + l]))
+        stores[-1].start()
     w.drain()
+    for store in stores:
+        store.wait()
 
 
 PANEL = 32
@@ -478,6 +502,17 @@
         a_ref[rest:, :] = old - change[rest - base :, :]
 
 
+def hand_over(a, b, c, a_out, b_out, c_out, sems):
+    copies = [
+        pltpu.make_async_copy(source.at[l], target.at[l], sems.at[n, l])
+        for n, (source, target) in enumerate(((a, a_out), (b, b_out), (c, c_out))) for l in range(LAYERS)
+    ]
+    for copy in copies:
+        copy.start()
+    for copy in copies:
+        copy.wait()
+
+
 def vmem(*shape):
     return pltpu.VMEM(shape, F32)
 
@@ -492,12 +527,13 @@
     share = basis.shape[1]
     whole = jax.ShapeDtypeStruct((LAYERS, rows, cols), F32)
     plane = [vmem(ZS, XS, share, RANK), vmem(XS, ZS, share, RANK), vmem(XS, ZS, share, RANK)]
-    sums = [vmem(2, RANK // 8, 8, HALF), vmem(2, RANK // 8, 8, HALF), vmem(ZS, 8, HALF), vmem(XS, 8, HALF)]
-    return pl.pallas_call(
+    sums = [vmem(4, HALF // 8, 8, HALF), vmem(4, HALF // 8, 8, HALF), vmem(ZS, 8, HALF), vmem(XS, 8, HALF)]
+    shapes = (whole, jax.ShapeDtypeStruct((LAYERS, share, RANK), F32), whole)
+    results = pl.pallas_call(
         kernel,
-        out_shape=(whole, jax.ShapeDtypeStruct((LAYERS, share, RANK), F32), whole),
+        out_shape=shapes,
         in_specs=[ANY, ANY, V],
-        out_specs=(V, V, V),
+        out_specs=(ANY, V, ANY),
         scratch_shapes=[
             vmem(LAYERS, rows, cols), vmem(LAYERS, rows, cols), *plane,
             vmem(LAYERS, YS, rows // YS, RANK), vmem(TP, rows // YS, RANK), vmem(LAYERS, YS, rows // YS, RANK),
@@ -507,13 +543,22 @@
             vmem(ZS, XS, share, RANK), vmem(XS, ZS, share, RANK), vmem(ZS, share, RANK), *plane,
             vmem(2, 8, XS, share, RANK), vmem(XS, share, RANK), vmem(2, 8, share, RANK),
             vmem(ZS, share, RANK), vmem(2, ZS, share, RANK),
-            vmem(ZS, XS, share, RANK), vmem(XS, ZS, share, RANK), vmem(TP, LAYERS, 8, RANK),
-            pltpu.SemaphoreType.DMA((COPIES,)), pltpu.SemaphoreType.DMA((COPIES,)), pltpu.SemaphoreType.DMA((2,)),
+            vmem(ZS, XS, share, RANK), vmem(XS, ZS, share, RANK), vmem(TP, LAYERS, 8, RANK), vmem(LAYERS, rows, cols),
+            pltpu.SemaphoreType.DMA((COPIES,)), pltpu.SemaphoreType.DMA((COPIES,)), pltpu.SemaphoreType.DMA((6,)),
         ],
         compiler_params=pltpu.CompilerParams(
             collective_id=0, has_side_effects=True, vmem_limit_bytes=60 * 2**20),
         name="step",
     )(gradient, momentum, basis)
+    return pl.pallas_call(
+        hand_over,
+        out_shape=shapes,
+        in_specs=[ANY] * 3,
+        out_specs=(ANY,) * 3,
+        scratch_shapes=[pltpu.SemaphoreType.DMA((3, LAYERS))],
+        compiler_params=pltpu.CompilerParams(vmem_limit_bytes=60 * 2**20),
+        name="hand_over",
+    )(*results)
 
 
 def solution(mesh):

time: 165 us -> 224 us (1.36)
  Pallas kernels: 160 us -> 223 us
  local copies, waits for them, and re-layouts: 3.99 us -> 0 us
    pallas_call x1 -> x2, Pallas kernels: 160 us -> 223 us  [the longest x1 157 us: per_device(): pl.pallas_call(kernel, out_shape=shapes, in_specs=[ANY, ANY, V], out_spec...]
    unnamed x7 -> x0, local copies, waits for them, and re-layouts: 3.99 us -> none
where the time goes in v5:
time: 224 us
  Pallas kernels  223 us (100%)
    pallas_call x1, Pallas kernels, per_device(): pl.pallas_call(kernel, out_shape=shapes, in_specs=[ANY, ANY, V], out_spec...  157 us
    pallas_call x1, Pallas kernels, per_device(): pl.pallas_call(hand_over, out_shape=shapes, in_specs=[ANY] * 3, out_specs...  65.7 us

profile of v5, /device:TPU:1, one launch (start us, length us, event | category | flops | bytes accessed | tf_op | source)
XLA Modules:
  0.0 223.9 jit_solution(3160094486087050433)
XLA Ops:
  0.6 157.4 %step.1 = (f32[2,128,1024]{2,1,0:T(8,128)}, f32[2,16,256]{2,1,0:T(8,128)}, f32[2,128,1024]{2,1,0:T(8,128)}) custom-call(f32[2,128,1024]{2,1,0:T(8,128)} %grad.1, f32[2,128,1024]{2,1,0:T(8,128)} %mom.1, f32[2,16,256]{2,1,0:T(8,128)} %basis.1), custom_call_target="tpu_custom_call" | custom-call | tf_op jit(solution)/shard_map/step/pallas_call | solution.py:532
  158.0 65.7 %hand_over.1 = (f32[2,128,1024]{2,1,0:T(8,128)}, f32[2,16,256]{2,1,0:T(8,128)}, f32[2,128,1024]{2,1,0:T(8,128)}) custom-call(f32[2,128,1024]{2,1,0:T(8,128)} %get-tuple-element.6.a, f32[2,16,256]{2,1,0:T(8,128)} %get-tuple-element.7.b, f32[2,128,1024]{2,1,0:T(8,128)} %get-tuple-element.8.c), custom_call_target="tpu_custom_call" | custom-call | tf_op jit(solution)/shard_map/hand_over/pallas_call | solution.py:553

commit v6 on v5

--- a/solution.py
+++ b/solution.py
@@ -117,11 +117,15 @@
     return 0 if d == 0 else 2 * d - 1 if way == 1 else 2 * d
 
 
-def offset(slot):
-    return 0 if slot == 0 else -((slot + 1) // 2) if slot % 2 else slot // 2
-
-
-GROUPS = ((0, 5), (5, 9), (9, 13), (13, 16))
+STREAMS = {0: ((1, 2), (-1, 2)), -5: ((1, 3), (-1, 2)), 5: ((1, 2), (-1, 2))}
+
+
+def slot_of(c, way, d):
+    return 15 if d == 3 else {0: 0, -5: 5, 5: 10}[c] + near(way, d)
+
+
+OFFSETS = {slot_of(c, way, d): c - way * d for c in STREAMS for way, hops in STREAMS[c] for d in range(hops + 1)}
+GROUPS = ((0, 5), (5, 10), (10, 16))
 
 
 def gather_plane(me, w, own0, own1, full0, slots1, full1, beside):
@@ -130,34 +134,47 @@
     full1[0, me.z] = own1
     xa = {e: w.go(full0.at[me.z, 0], full0.at[me.z, (-e) % XS], me.xdev(e)) for e in (3, 1, 2)}
     ring, wide, ahead = {}, {}, {}
+    for c in (-5, 5):
+        ring["b", c] = w.go(slots1.at[0, 0], slots1.at[0, slot_of(c, 1, 0)], me.zdev(-c))
 
     def hop_b(s):
-        for way, last in WAYS:
-            if 0 < s <= last:
-                ring["b", way, s - 1].wait_recv()
-            if s < last:
-                ring["b", way, s] = w.go(
-                    slots1.at[0, near(way, s)], slots1.at[0, near(way, s + 1)], me.zdev(way))
+        for c, ways in STREAMS.items():
+            i = s if c == 0 else s - 2
+            if i == 0 and c != 0:
+                ring["b", c].wait_recv()
+            for way, last in ways:
+                if 0 < i <= last:
+                    ring["b", c, way, i - 1].wait_recv()
+                if 0 <= i < last:
+                    ring["b", c, way, i] = w.go(
+                        slots1.at[0, slot_of(c, way, i)], slots1.at[0, slot_of(c, way, i + 1)], me.zdev(way))
 
     def hop_a(s):
         for half in (0, 1):
             pair = pl.ds(2 * half, 2)
-            for way, last in WAYS:
-                if s == 0 and way == 1:
-                    for e in ((3,), (1, 2))[half]:
-                        xa[e].wait_recv()
-                if 0 < s <= last:
-                    ring["a", way, s - 1, half].wait_recv()
-                if s < last:
-                    block = full0.at[me.zat(-way * s), pair]
-                    ring["a", way, s, half] = w.go(block, block, me.zdev(way))
+            if s == 0:
+                for e in ((3,), (1, 2))[half]:
+                    xa[e].wait_recv()
+                block = full0.at[me.z, pair]
+                for c in (-5, 5):
+                    ring["a", c, half] = w.go(block, block, me.zdev(-c))
+            for c, ways in STREAMS.items():
+                i = s if c == 0 else s - 3
+                if i == 0 and c != 0:
+                    ring["a", c, half].wait_recv()
+                for way, last in ways:
+                    if 0 < i <= last:
+                        ring["a", c, way, i - 1, half].wait_recv()
+                    if 0 <= i < last:
+                        block = full0.at[me.zat(c - way * i), pair]
+                        ring["a", c, way, i, half] = w.go(block, block, me.zdev(way))
 
     def spread(g):
         lo, hi = GROUPS[g]
         group = slots1.at[0, pl.ds(lo, hi - lo)]
         wide[g] = [w.go(group, slots1.at[(-e) % XS, pl.ds(lo, hi - lo)], me.xdev(e)) for e in (1, -1)]
         for i in range(lo, hi):
-            full1[0, me.zat(offset(i))] = slots1[0, i]
+            full1[0, me.zat(OFFSETS[i])] = slots1[0, i]
 
     def forward(g):
         lo, hi = GROUPS[g]
@@ -169,24 +186,24 @@
                 w.go(slots1.at[(-e) % XS, pl.ds(a, b - a)], slots1.at[2, pl.ds(a, b - a)], me.xdev(e)))
         for i in range(lo, hi):
             for e in (1, 3):
-                full1[e, me.zat(offset(i))] = slots1[e, i]
-
-    for s in range(9):
+                full1[e, me.zat(OFFSETS[i])] = slots1[e, i]
+
+    for s in range(7):
         hop_b(s)
-        if s in (2, 4, 6, 8):
-            spread(s // 2 - 1)
+        if s in (2, 4, 5):
+            spread((2, 4, 5).index(s))
         hop_a(s)
-        if s in (4, 6, 8):
+        if s in (4, 6):
             forward(s // 2 - 2)
         beside(s)
         w.drain(64)
-    forward(3)
+    forward(2)
     beside(9)
-    for g in range(4):
+    for g in range(3):
         for copy in ahead[g]:
             copy.wait_recv()
         for i in range(*GROUPS[g]):
-            full1[2, me.zat(offset(i))] = slots1[2, i]
+            full1[2, me.zat(OFFSETS[i])] = slots1[2, i]
 
 
 FAR = [8] + [d for r in range(7, 0, -1) for d in (r, -r)] + [0]
@@ -396,13 +413,9 @@
             next(sums[1], None)
         if s == 5:
             take(gfull2)
-        for n in {5: (0,), 6: (1, 2, 3), 7: (4, 5, 6), 8: (7,)}.get(s, ()):
+        for n in {5: (0, 1), 6: (2, 3), 9: (4, 5, 6, 7)}.get(s, ()):
             eliminate(a, w2, n * PANEL)
         if s == 9:
-            for copy in trade:
-                copy.wait_recv()
-            finish(0)
-        if s == 8:
             wide[me.c] = dot(w2[...], w1[...], ((1,), (0,)))
             trade.append(w.go(wide.at[me.c], wide.at[me.c], me.cdev()))
             p2[me.c] = dot(p1[...], w2[...], ((1,), (1,)))
@@ -421,6 +434,9 @@
 
     own = scatter_plane(me, w, part0, part1, rb0, xb0, rb1, half1, whole1, fill0, fill1, beside_scatter)
     gather_plane(me, w, own[0], own[1], full0, slots1, full1, beside_gather)
+    for copy in trade:
+        copy.wait_recv()
+    finish(0)
     finish(1)
     stores = []
     copies = [w.go(sq.at[me.t], sq.at[me.t], me.tdev(d)) for d in range(1, TP)]
@@ -502,15 +518,10 @@
         a_ref[rest:, :] = old - change[rest - base :, :]
 
 
-def hand_over(a, b, c, a_out, b_out, c_out, sems):
-    copies = [
-        pltpu.make_async_copy(source.at[l], target.at[l], sems.at[n, l])
-        for n, (source, target) in enumerate(((a, a_out), (b, b_out), (c, c_out))) for l in range(LAYERS)
-    ]
-    for copy in copies:
-        copy.start()
-    for copy in copies:
-        copy.wait()
+def hand_over(a, b, c, a_out, b_out, c_out):
+    a_out[...] = a[...]
+    b_out[...] = b[...]
+    c_out[...] = c[...]
 
 
 def vmem(*shape):
@@ -553,9 +564,9 @@
     return pl.pallas_call(
         hand_over,
         out_shape=shapes,
-        in_specs=[ANY] * 3,
-        out_specs=(ANY,) * 3,
-        scratch_shapes=[pltpu.SemaphoreType.DMA((3, LAYERS))],
+        grid=(LAYERS,),
+        in_specs=[pl.BlockSpec((1,) + shape.shape[1:], lambda l: (l, 0, 0)) for shape in shapes],
+        out_specs=tuple(pl.BlockSpec((1,) + shape.shape[1:], lambda l: (l, 0, 0)) for shape in shapes),
         compiler_params=pltpu.CompilerParams(vmem_limit_bytes=60 * 2**20),
         name="hand_over",
     )(*results)

time: 224 us -> 159 us (0.71)
  Pallas kernels: 223 us -> 158 us
    pallas_call x1, Pallas kernels: 65.7 us -> 2.62 us  [per_device(): pl.pallas_call(hand_over, out_shape=shapes, grid=(LAYERS,), in_specs=[pl....]
where the time goes in v6:
time: 159 us; the launch traced here: 158 us
  Pallas kernels  158 us (99%)
    pallas_call x1, Pallas kernels, per_device(): pl.pallas_call(kernel, out_shape=shapes, in_specs=[ANY, ANY, V], out_spec...  155 us

profile of v6, /device:TPU:1, one launch (start us, length us, event | category | flops | bytes accessed | tf_op | source)
XLA Modules:
  0.0 158.4 jit_solution(15604451747580354415)
XLA Ops:
  0.6 155.2 %step.1 = (f32[2,128,1024]{2,1,0:T(8,128)}, f32[2,16,256]{2,1,0:T(8,128)}, f32[2,128,1024]{2,1,0:T(8,128)}) custom-call(f32[2,128,1024]{2,1,0:T(8,128)} %grad.1, f32[2,128,1024]{2,1,0:T(8,128)} %mom.1, f32[2,16,256]{2,1,0:T(8,128)} %basis.1), custom_call_target="tpu_custom_call" | custom-call | tf_op jit(solution)/shard_map/step/pallas_call | solution.py:543
  155.8 2.6 %hand_over.1 = (f32[2,128,1024]{2,1,0:T(8,128)}, f32[2,16,256]{2,1,0:T(8,128)}, f32[2,128,1024]{2,1,0:T(8,128)}) custom-call(f32[2,128,1024]{2,1,0:T(8,128)} %get-tuple-element.6.a, f32[2,16,256]{2,1,0:T(8,128)} %get-tuple-element.7.b, f32[2,128,1024]{2,1,0:T(8,128)} %get-tuple-element.8.c), custom_call_target="tpu_custom_call" | custom-call | tf_op jit(solution)/shard_map/hand_over/pallas_call | solution.py:564

commit v7 on v6

--- a/solution.py
+++ b/solution.py
@@ -331,7 +331,7 @@
 
 
 def kernel(grad, mom, basis, new_mom, new_basis, update,
-           gbuf, mbuf, bfull0, bslots1, bfull1, part, rs, q, p1, p2, a, w1, w2, wide,
+           gbuf, mbuf, bfull0, bslots1, bfull1, part, rs, q, p1, p2, a, w1, w2, turned,
            gs, gfull, zbuf, xbuf, gs2, gfull2, zbuf2, xbuf2,
            part0, part1, tmp, full0, slots1, full1, rb0, xb0, rb1, half1, whole1, cols0, cols1, sq, out,
            send, recv, local):
@@ -355,6 +355,8 @@
             for load in loads:
                 load.wait()
             gbuf[...] = gbuf[...] + mbuf[...]
+        if s in (1, 2):
+            turned[s - 1] = gbuf[s - 1].T
         if s == 9:
             multiply(0)
 
@@ -387,11 +389,11 @@
 
     def fill0():
         for e in range(XS):
-            cols = dot(gbuf[0, :, me.cols(e)], q[0].reshape(YS * share, RANK), ((0,), (0,)))
+            cols = dot(turned[0, me.cols(e)], q[0].reshape(YS * share, RANK), ((1,), (0,)))
             part0[:, e] = cols.reshape(ZS, 16, RANK)
 
     def fill1(e):
-        cols = dot(gbuf[1, :, me.cols(e)], q[1].reshape(YS * share, RANK), ((0,), (0,)))
+        cols = dot(turned[1, me.cols(e)], q[1].reshape(YS * share, RANK), ((1,), (0,)))
         tmp[...] = cols.reshape(ZS, 16, RANK)
         for slot, d in enumerate(FAR):
             part1[e, slot] = tmp[me.zat(d)]
@@ -402,29 +404,29 @@
         if s == 6:
             take(gfull)
         for n in {7: (0, 1, 2), 8: (3, 4, 5), 9: (6, 7)}.get(s, ()):
-            eliminate(a, w1, n * PANEL)
+            eliminate(a, w1.at[me.c], n * PANEL)
         if s == 9:
-            p1[...] = dot(q[me.c].reshape(YS * share, RANK), w1[...], ((1,), (1,)))
+            trade.append(w.go(w1.at[me.c], w1.at[me.c], me.cdev()))
+            p1[...] = dot(q[me.c].reshape(YS * share, RANK), w1[me.c], ((1,), (1,)))
             sums.append(sum_gram(me, w, p1[...], gs2, gfull2, zbuf2, xbuf2))
             next(sums[1])
 
     def beside_gather(s):
-        if s in (0, 1, 3, 5):
+        if s in (0, 1, 2, 4):
             next(sums[1], None)
-        if s == 5:
+        if s == 4:
             take(gfull2)
-        for n in {5: (0, 1), 6: (2, 3), 9: (4, 5, 6, 7)}.get(s, ()):
-            eliminate(a, w2, n * PANEL)
+        for n in {4: (0, 1), 5: (2, 3), 6: (4, 5), 9: (6, 7)}.get(s, ()):
+            eliminate(a, w2.at[me.c], n * PANEL)
         if s == 9:
-            wide[me.c] = dot(w2[...], w1[...], ((1,), (0,)))
-            trade.append(w.go(wide.at[me.c], wide.at[me.c], me.cdev()))
-            p2[me.c] = dot(p1[...], w2[...], ((1,), (1,)))
+            trade.append(w.go(w2.at[me.c], w2.at[me.c], me.cdev()))
+            p2[me.c] = dot(p1[...], w2[me.c], ((1,), (1,)))
             trade.append(w.go(p2.at[me.c], p2.at[me.c], me.cdev()))
 
     def finish(l):
         squares = jnp.zeros((1, RANK), F32)
         for e in range(XS):
-            block = dot(gathered(full0, full1, l, e), wide[l], ((1,), (1,)))
+            block = dot3(gathered(full0, full1, l, e), w2[l], 1)
             if l == 0:
                 cols0[:, e] = block.reshape(ZS, 16, RANK)
             else:
@@ -433,8 +435,10 @@
         sq[me.t, l] = jnp.broadcast_to(squares, (8, RANK))
 
     own = scatter_plane(me, w, part0, part1, rb0, xb0, rb1, half1, whole1, fill0, fill1, beside_scatter)
+    trade[0].wait_recv()
+    own = [dot(own[l], w1[l], ((1,), (1,))) for l in range(LAYERS)]
     gather_plane(me, w, own[0], own[1], full0, slots1, full1, beside_gather)
-    for copy in trade:
+    for copy in trade[1:]:
         copy.wait_recv()
     finish(0)
     finish(1)
@@ -549,7 +553,7 @@
             vmem(LAYERS, rows, cols), vmem(LAYERS, rows, cols), *plane,
             vmem(LAYERS, YS, rows // YS, RANK), vmem(TP, rows // YS, RANK), vmem(LAYERS, YS, rows // YS, RANK),
             vmem(rows, RANK), vmem(LAYERS, rows, RANK),
-            vmem(RANK, RANK), vmem(RANK, RANK), vmem(RANK, RANK), vmem(LAYERS, RANK, RANK),
+            vmem(RANK, RANK), vmem(LAYERS, RANK, RANK), vmem(LAYERS, RANK, RANK), vmem(LAYERS, cols, rows),
             *sums, *sums,
             vmem(ZS, XS, share, RANK), vmem(XS, ZS, share, RANK), vmem(ZS, share, RANK), *plane,
             vmem(2, 8, XS, share, RANK), vmem(XS, share, RANK), vmem(2, 8, share, RANK),

time: 159 us -> 157 us (0.987)
  Pallas kernels: 158 us -> 156 us
    pallas_call x1, Pallas kernels: 155 us -> 153 us  [per_device(): pl.pallas_call(kernel, out_shape=shapes, in_specs=[ANY, ANY, V], out_spec...]
where the time goes in v7:
time: 157 us
  Pallas kernels  156 us (99%)
    pallas_call x1, Pallas kernels, per_device(): pl.pallas_call(kernel, out_shape=shapes, in_specs=[ANY, ANY, V], out_spec...  153 us

profile of v7, /device:TPU:1, one launch (start us, length us, event | category | flops | bytes accessed | tf_op | source)
XLA Modules:
  0.0 156.7 jit_solution(1146045733074158534)
XLA Ops:
  0.6 153.4 %step.1 = (f32[2,128,1024]{2,1,0:T(8,128)}, f32[2,16,256]{2,1,0:T(8,128)}, f32[2,128,1024]{2,1,0:T(8,128)}) custom-call(f32[2,128,1024]{2,1,0:T(8,128)} %grad.1, f32[2,128,1024]{2,1,0:T(8,128)} %mom.1, f32[2,16,256]{2,1,0:T(8,128)} %basis.1), custom_call_target="tpu_custom_call" | custom-call | tf_op jit(solution)/shard_map/step/pallas_call | solution.py:547
  154.0 2.6 %hand_over.1 = (f32[2,128,1024]{2,1,0:T(8,128)}, f32[2,16,256]{2,1,0:T(8,128)}, f32[2,128,1024]{2,1,0:T(8,128)}) custom-call(f32[2,128,1024]{2,1,0:T(8,128)} %get-tuple-element.6.a, f32[2,16,256]{2,1,0:T(8,128)} %get-tuple-element.7.b, f32[2,128,1024]{2,1,0:T(8,128)} %get-tuple-element.8.c), custom_call_target="tpu_custom_call" | custom-call | tf_op jit(solution)/shard_map/hand_over/pallas_call | solution.py:568

commit v8 on v7

--- a/solution.py
+++ b/solution.py
@@ -401,27 +401,33 @@
     def beside_scatter(s):
         if s in (1, 2, 4, 6):
             next(sums[0], None)
+        if s == 10:
+            next(sums[1])
         if s == 6:
             take(gfull)
-        for n in {7: (0, 1, 2), 8: (3, 4, 5), 9: (6, 7)}.get(s, ()):
+        for n in {6: (0, 1), 7: (2, 3, 4), 8: (5, 6, 7)}.get(s, ()):
             eliminate(a, w1.at[me.c], n * PANEL)
-        if s == 9:
+        if s == 8:
             trade.append(w.go(w1.at[me.c], w1.at[me.c], me.cdev()))
             p1[...] = dot(q[me.c].reshape(YS * share, RANK), w1[me.c], ((1,), (1,)))
             sums.append(sum_gram(me, w, p1[...], gs2, gfull2, zbuf2, xbuf2))
             next(sums[1])
 
     def beside_gather(s):
-        if s in (0, 1, 2, 4):
+        if s in (0, 2, 4):
             next(sums[1], None)
         if s == 4:
             take(gfull2)
-        for n in {4: (0, 1), 5: (2, 3), 6: (4, 5), 9: (6, 7)}.get(s, ()):
+        for n in {4: (0, 1, 2), 5: (3, 4, 5), 6: (6, 7)}.get(s, ()):
             eliminate(a, w2.at[me.c], n * PANEL)
-        if s == 9:
+        if s == 6:
             trade.append(w.go(w2.at[me.c], w2.at[me.c], me.cdev()))
             p2[me.c] = dot(p1[...], w2[me.c], ((1,), (1,)))
             trade.append(w.go(p2.at[me.c], p2.at[me.c], me.cdev()))
+        if s == 9:
+            for copy in trade[1:]:
+                copy.wait_recv()
+            finish(0)
 
     def finish(l):
         squares = jnp.zeros((1, RANK), F32)
@@ -438,9 +444,6 @@
     trade[0].wait_recv()
     own = [dot(own[l], w1[l], ((1,), (1,))) for l in range(LAYERS)]
     gather_plane(me, w, own[0], own[1], full0, slots1, full1, beside_gather)
-    for copy in trade[1:]:
-        copy.wait_recv()
-    finish(0)
     finish(1)
     stores = []
     copies = [w.go(sq.at[me.t], sq.at[me.t], me.tdev(d)) for d in range(1, TP)]

time: 157 us -> 156 us (level)
  no operation moved by 1% of the time
where the time goes in v8:
time: 156 us; the launch traced here: 155 us
  Pallas kernels  155 us (99%)
    pallas_call x1, Pallas kernels, per_device(): pl.pallas_call(kernel, out_shape=shapes, in_specs=[ANY, ANY, V], out_spec...  152 us

profile of v8, /device:TPU:1, one launch (start us, length us, event | category | flops | bytes accessed | tf_op | source)
XLA Modules:
  0.0 155.5 jit_solution(9066130623053271170)
XLA Ops:
  0.6 152.2 %step.1 = (f32[2,128,1024]{2,1,0:T(8,128)}, f32[2,16,256]{2,1,0:T(8,128)}, f32[2,128,1024]{2,1,0:T(8,128)}) custom-call(f32[2,128,1024]{2,1,0:T(8,128)} %grad.1, f32[2,128,1024]{2,1,0:T(8,128)} %mom.1, f32[2,16,256]{2,1,0:T(8,128)} %basis.1), custom_call_target="tpu_custom_call" | custom-call | tf_op jit(solution)/shard_map/step/pallas_call | solution.py:550
  152.8 2.6 %hand_over.1 = (f32[2,128,1024]{2,1,0:T(8,128)}, f32[2,16,256]{2,1,0:T(8,128)}, f32[2,128,1024]{2,1,0:T(8,128)}) custom-call(f32[2,128,1024]{2,1,0:T(8,128)} %get-tuple-element.6.a, f32[2,16,256]{2,1,0:T(8,128)} %get-tuple-element.7.b, f32[2,128,1024]{2,1,0:T(8,128)} %get-tuple-element.8.c), custom_call_target="tpu_custom_call" | custom-call | tf_op jit(solution)/shard_map/hand_over/pallas_call | solution.py:571
